TPU v7x, 128 devices: a whole 4x4x4 slice. The times are simulated.
128 devices in a mesh: batch: 8 (over z, core), ctx: 16 (over y, x).
Axes of the slice: x: 4, y: 4, z: 4, core: 2. Of those that a mesh axis runs over, the one named last changes fastest.
Arguments:
- tokens: bfloat16 [16384, 7168], P(('batch', 'ctx')), may hold values from -6 to 6
- q_latent: bfloat16 [16384, 1536], P(('batch', 'ctx')), may hold values from -102 to 102
- w_down_kv: bfloat16 [7168, 512], P(('batch', 'ctx')), may hold values from -0.0625 to 0.0625
- w_down_rope: bfloat16 [64, 7168], P(None, ('batch', 'ctx')), may hold values from -0.0625 to 0.0625
- kv_gain: float32 [512], replicated, may hold values from 0.1 to 1.9
- w_up_q: bfloat16 [1536, 18432], P('batch', 'ctx'), may hold values from -0.15625 to 0.15625
- w_up_kv: bfloat16 [512, 24576], P('batch', 'ctx'), may hold values from -0.25 to 0.25
- lengths: int32 [8, 4], P('batch'), may hold values from 1 to 8, 16 in all within a row
- window: int32 [8, 4], P('batch'), may hold values from 1 to 4, as said below
- flags: int32 [8, 4], P('batch'), may hold values 0 or 1
- anchor_pick: int32 [8, 4], P('batch'), may hold values from 0 to 65535
Outputs:
- attended: bfloat16 [16384, 12288], P(('batch', 'ctx'))
Inputs may be any that keep to these rules, and one draw needn't show every extreme that they name: Each pack's lengths sum to 16, and some stream has exactly 8 blocks. Every pack has a stream with window 4.
All inputs are finite; a program needn't handle non-finite values. No bound on the sum of `flags` on one device may be relied on, other than what follows from the above.
Results may differ from a plain program's by a relative error of at most 0.015.
The roundings to bfloat16 on the way count: a program that leaves them out, or rounds other values in their place, can miss the bound.
Values may be sent and summed in bfloat16 or wider, within the bound.
A program may use at most 128 MiB of HBM per device.

v0:
```python
import math

import jax
import jax.numpy as jnp
from jax import lax
from jax.sharding import PartitionSpec as P

NOPE = 128
ROPE = 64
VDIM = 128
BLK = 128


def angles(positions):
    half_dim = ROPE // 2
    freq = jnp.exp(-math.log(10000.0) * 2.0 * jnp.arange(half_dim, dtype=jnp.float32) / ROPE)
    phase = positions[:, None] * freq[None, :]
    return (jnp.cos(phase), jnp.sin(phase))


def rotate(values, cosine, sine):
    half_dim = ROPE // 2
    first = values[..., :half_dim]
    second = values[..., half_dim:]
    return jnp.concatenate(
        [first * cosine - second * sine, first * sine + second * cosine], axis=-1
    )


def rotate_rows(values, cosine, sine):
    half_dim = ROPE // 2
    first = values[:half_dim]
    second = values[half_dim:]
    return jnp.concatenate([first * cosine - second * sine, first * sine + second * cosine], axis=0)


def lookup(streams, table):
    slots = jnp.arange(table.shape[0], dtype=jnp.int32)
    onehot = (streams[:, None] == slots[None, :]).astype(jnp.int32)
    return jnp.sum(onehot * table[None, :], axis=1)


def stream_of(blocks, ends):
    return jnp.sum((ends[None, :] <= blocks[:, None]).astype(jnp.int32), axis=1)


def allowed(query_ids, key_ids, tables):
    ends, window_len, flag_set, anchors = tables
    query_blocks = query_ids // BLK
    key_blocks = key_ids // BLK
    query_streams = stream_of(query_blocks, ends)
    key_streams = stream_of(key_blocks, ends)
    same = query_streams[:, None] == key_streams[None, :]
    causal = key_ids[None, :] <= query_ids[:, None]
    near = query_blocks[:, None] - key_blocks[None, :] < lookup(query_streams, window_len)[:, None]
    anchored = (lookup(query_streams, flag_set)[:, None] == 1) & (
        key_blocks[None, :] == lookup(query_streams, anchors)[:, None]
    )
    return same & causal & (near | anchored)


def attend(query_tile, key_nope, key_rope, values, mask):
    scale = (NOPE + ROPE) ** (-0.5)
    scores = jnp.einsum(
        "qhd,khd->hqk", query_tile[..., :NOPE], key_nope, preferred_element_type=jnp.float32
    )
    scores = (
        scores
        + jnp.einsum(
            "qhd,dk->hqk", query_tile[..., NOPE:], key_rope, preferred_element_type=jnp.float32
        )
    ) * scale
    scores = jnp.where(mask[None], scores, -1e30)
    maxima = jnp.max(scores, axis=-1, keepdims=True)
    weights = jnp.where(mask[None], jnp.exp(scores - maxima), 0.0)
    totals = jnp.sum(weights, axis=-1)
    mixed = jnp.einsum(
        "hqk,khd->qhd", weights.astype(jnp.bfloat16), values, preferred_element_type=jnp.float32
    )
    return (mixed / jnp.transpose(totals)[:, :, None]).astype(jnp.bfloat16)


def per_device(
    tokens,
    q_latent,
    w_down_kv,
    w_down_rope,
    kv_gain,
    w_up_q,
    w_up_kv,
    lengths,
    window,
    flags,
    anchor_pick,
):
    n_ctx = lax.axis_size("ctx")
    tok_dev = tokens.shape[0]
    pack_rows = tok_dev * n_ctx
    ctx_index = lax.axis_index("ctx")
    stream_len = lengths[0]
    ends = jnp.cumsum(stream_len)
    starts = ends - stream_len
    anchors = starts + anchor_pick[0] % stream_len
    tables = (ends, window[0], flags[0], anchors)

    def positions_of(row_ids):
        streams = stream_of(row_ids // BLK, ends)
        return (row_ids - lookup(streams, starts) * BLK).astype(jnp.float32)

    columns = tokens
    latent = jnp.dot(
        columns,
        lax.all_gather(w_down_kv, ("batch", "ctx"), axis=0, tiled=True),
        preferred_element_type=jnp.float32,
    )
    columns = tokens
    rope_part = lax.dot_general(
        lax.all_gather(w_down_rope, ("batch", "ctx"), axis=1, tiled=True),
        columns,
        (((1,), (1,)), ((), ())),
        preferred_element_type=jnp.float32,
    )
    own_rows = ctx_index * tok_dev + jnp.arange(tok_dev, dtype=jnp.int32)
    cosine, sine = angles(positions_of(own_rows))
    kv_normed = (
        latent * lax.rsqrt(jnp.mean(latent * latent, axis=-1, keepdims=True) + 1e-06) * kv_gain
    ).astype(jnp.bfloat16)
    key_rope = rotate_rows(rope_part, jnp.transpose(cosine), jnp.transpose(sine)).astype(
        jnp.bfloat16
    )
    kv_all, rope_all = (
        lax.all_gather(kv_normed, "ctx", axis=0, tiled=True),
        lax.all_gather(key_rope, "ctx", axis=1, tiled=True),
    )
    query_up, keyval_up = (
        lax.all_gather(w_up_q, "batch", axis=0, tiled=True),
        lax.all_gather(w_up_kv, "batch", axis=0, tiled=True),
    )
    local_heads = query_up.shape[1] // (NOPE + ROPE)
    pieces = lax.all_gather(q_latent, "ctx", axis=0, tiled=True)
    count = pieces.shape[0]
    row_ids = jnp.arange(count, dtype=jnp.int32)
    row_cos, row_sin = angles(positions_of(row_ids))
    projected = jnp.dot(pieces, query_up, preferred_element_type=jnp.float32).reshape(
        count, local_heads, NOPE + ROPE
    )
    projected = jnp.concatenate(
        [
            projected[..., :NOPE],
            rotate(projected[..., NOPE:], row_cos[:, None, :], row_sin[:, None, :]),
        ],
        axis=-1,
    )
    query = (
        projected.reshape(count, local_heads * (NOPE + ROPE))
        .astype(jnp.bfloat16)
        .reshape(pack_rows, local_heads, NOPE + ROPE)
    )
    keyval = (
        jnp.dot(kv_all, keyval_up, preferred_element_type=jnp.float32)
        .astype(jnp.bfloat16)
        .reshape(pack_rows, local_heads, NOPE + VDIM)
    )
    tile_rows = 4 * BLK
    key_ids = jnp.arange(pack_rows, dtype=jnp.int32)

    def one_tile(tile_index):
        first_row = tile_index * tile_rows
        query_tile = lax.dynamic_slice_in_dim(query, first_row, tile_rows, 0)
        query_ids = first_row + jnp.arange(tile_rows, dtype=jnp.int32)
        mask = allowed(query_ids, key_ids, tables)
        return attend(query_tile, keyval[..., :NOPE], rope_all, keyval[..., NOPE:], mask)

    outputs = lax.map(one_tile, jnp.arange(pack_rows // tile_rows, dtype=jnp.int32))
    outputs = outputs.reshape(pack_rows, local_heads * VDIM)
    return lax.all_to_all(outputs, "ctx", split_axis=0, concat_axis=1, tiled=True)


def solution(mesh):
    return jax.shard_map(
        per_device,
        mesh=mesh,
        in_specs=(
            P(("batch", "ctx"), None),
            P(("batch", "ctx"), None),
            P(("batch", "ctx"), None),
            P(None, ("batch", "ctx")),
            P(),
            P("batch", "ctx"),
            P("batch", "ctx"),
            P("batch", None),
            P("batch", None),
            P("batch", None),
            P("batch", None),
        ),
        out_specs=P(("batch", "ctx"), None),
        check_vma=False,
    )
```

profile of v0, /device:TPU:0, one launch (start us, length us, event | category | flops | bytes accessed | tf_op | source)
XLA Modules:
  0.0 523.3 jit_solution(9275882966746812305)
XLA Ops:
  11.1 72.1 %all_gather.26 = bf16[64,7168]{0,1:T(8,128)(2,1)S(1)} all-gather(bf16[64,56]{0,1:T(8,128)(2,1)} %param.16), channel_id=1, replica_groups=mesh['batch'=8,'ctx'=16] {'batch','ctx'}, dimensions={1}, use_global_device_ids=true | all-gather | bytes 924672 | tf_op jit(solution)/shard_map/all_gather | solution.py:118
  84.0 23.8 %all_gather.27 = bf16[64,2048]{1,0:T(8,128)(2,1)S(1)} all-gather(bf16[64,128]{1,0:T(8,128)(2,1)S(1)} %pad_maximum_fusion.1), channel_id=1, replica_groups=mesh['batch'=8,'ctx'=16] {'ctx'}, dimensions={1}, use_global_device_ids=true | all-gather | bytes 278528 | tf_op jit(solution)/shard_map/all_gather | solution.py:133
  108.1 4.4 multiply_reduce_fusion
  114.4 60.9 %all-gather.6.cloned.1.call-done = bf16[2048,1536]{1,0:T(8,128)(2,1)} async-done(((bf16[128,1536]{1,0:T(8,128)(2,1)}), bf16[2048,1536]{1,0:T(8,128)(2,1)}) %all-gather.6.cloned.1.call-update) | async-done | bytes 6291472 | tf_op jit(solution)/shard_map/all_gather | solution.py:140
  175.3 11.1 %fusion.65 = f32[2048,1152]{0,1:T(8,128)S(1)} fusion(bf16[2048,1536]{1,0:T(8,128)(2,1)} %all-gather.6.cloned.1.call-done, bf16[1536,1152]{1,0:T(8,128)(2,1)} %all-gather.8.cloned.1.call-done), kind=kOutput, calls=%fused_computation.103 | convolution fusion | flops 7247757312 | bytes 19267584 | tf_op jit(solution)/shard_map/dot_general | solution.py:144
  187.4 2.5 pad_maximum_fusion
  189.9 11.3 %all-gather.14.cloned.1.call-done = bf16[512,1536]{1,0:T(8,128)(2,1)} async-done(((bf16[64,1536]{1,0:T(8,128)(2,1)}), bf16[512,1536]{1,0:T(8,128)(2,1)}) %all-gather.14.cloned.1.call-update) | async-done | bytes 1572880 | tf_op jit(solution)/shard_map/all_gather | solution.py:137
  201.2 46.9 %all-gather.12.cloned.1.call-done = bf16[2048,512]{1,0:T(8,128)(2,1)} async-done(((bf16[128,512]{1,0:T(8,128)(2,1)}), bf16[2048,512]{1,0:T(8,128)(2,1)}) %all-gather.12.cloned.1.call-update) | async-done | bytes 2097168 | tf_op jit(solution)/shard_map/all_gather | solution.py:132
  248.0 8.2 %convolution_convert_fusion = bf16[2048,1536]{0,1:T(8,128)(2,1)} fusion(bf16[2048,512]{1,0:T(8,128)(2,1)} %all-gather.12.cloned.1.call-done, bf16[512,1536]{1,0:T(8,128)(2,1)} %all-gather.14.cloned.1.call-done), kind=kOutput, calls=%fused_computation.54 | convolution fusion | flops 3224371200 | bytes 9961472 | tf_op jit(solution)/shard_map/dot_general | solution.py:160
  256.2 8.7 %copy.49 = bf16[2048,6,256]{2,0,1:T(8,128)(2,1)} copy(bf16[2048,6,256]{0,2,1:T(8,128)(2,1)} %bitcast.82) | data formatting | bytes 12582912
  264.9 188.7 %while.15 = (s32[]{:T(128)}, bf16[4,512,6,128]{3,1,2,0:T(8,128)(2,1)}, s32[4]{0:T(128)S(1)}, s32[4]{0:T(128)S(1)}, s32[1,4]{1,0:T(1,128)S(1)}, /*index=5*/s32[1,...) while((s32[]{:T(128)}, ...), condition=%wide.region_14.15_spmd.clone.clone, body=%wide.region_6.14_spmd.clone.clone.sunk | while | flops 4080880128 | bytes 87275312 | solution.py:174
  266.9 2.5 fusion.92
  269.4 13.9 %fusion.93 = f32[6,512,2048]{2,1,0:T(8,128)} fusion(bf16[2048,6,256]{2,0,1:T(8,128)(2,1)} %get-tuple-element.502, bf16[2048,6,192]{0,2,1:T(8,128)(2,1)} %get-tuple-element.501, s32[]{:T(128)S(6)} %select_n.126), kind=kOutput, calls=%fused_computation.18.clone.1 | convolution fusion | flops 1610612736 | bytes 29097988 | tf_op jit(solution)/shard_map/while/body/eval_jaxpr/qhd,khd->hqk/dot_general | solution.py:64
  283.3 19.2 %fusion.94 = (f32[6,512]{1,0:T(8,128)S(1)}, bf16[6,512,2048]{2,1,0:T(8,128)(2,1)}) fusion(pred[512,2048]{1,0:T(8,128)(4,1)S(1)} %fusion.92, f32[6,512,2048]{2,1,0:T(8,128)} %fusion.93, bf16[2048,6,192]{0,2,1:T(8,128)(2,1)} %get-tuple-element.501, s32[]{:T(128)S(6)} %select_n.126, s32[]{:T(128)S(6)} %add.191, ...), kind=kOutput, calls=%fused_computation.102.clone.1 | convolution fusion | flops 849348608 | bytes 40513544 | tf_op jit(solution)/shard_map/while/body/eval_jaxpr/sub | solution.py:75
  302.5 9.8 %fusion.95 = bf16[4,512,6,128]{3,1,2,0:T(8,128)(2,1)} fusion(bf16[4,512,6,128]{3,1,2,0:T(8,128)(2,1)} %get-tuple-element.480, s32[]{:T(128)} %get-tuple-element.479, bf16[2048,6,256]{2,0,1:T(8,128)(2,1)} %get-tuple-element.502, bf16[6,512,2048]{2,1,0:T(8,128)(2,1)} %get-tuple-element.462, f32[512,6]{0,1:T(8,128)S(1)} %bitcast.91), kind=kOutput, calls=%fused_computation.23.clone.1 | convolution fusion | flops 1611399168 | bytes 16527872 | tf_op jit(solution)/shard_map/while/body/eval_jaxpr/hqk,khd->qhd/dot_general | solution.py:77
  314.0 2.5 fusion.92
  316.5 13.9 %fusion.93 = f32[6,512,2048]{2,1,0:T(8,128)} fusion(bf16[2048,6,256]{2,0,1:T(8,128)(2,1)} %get-tuple-element.502, bf16[2048,6,192]{0,2,1:T(8,128)(2,1)} %get-tuple-element.501, s32[]{:T(128)S(6)} %select_n.126), kind=kOutput, calls=%fused_computation.18.clone.1 | convolution fusion | flops 1610612736 | bytes 29097988 | tf_op jit(solution)/shard_map/while/body/eval_jaxpr/qhd,khd->hqk/dot_general | solution.py:64
  330.4 19.2 %fusion.94 = (f32[6,512]{1,0:T(8,128)S(1)}, bf16[6,512,2048]{2,1,0:T(8,128)(2,1)}) fusion(pred[512,2048]{1,0:T(8,128)(4,1)S(1)} %fusion.92, f32[6,512,2048]{2,1,0:T(8,128)} %fusion.93, bf16[2048,6,192]{0,2,1:T(8,128)(2,1)} %get-tuple-element.501, s32[]{:T(128)S(6)} %select_n.126, s32[]{:T(128)S(6)} %add.191, ...), kind=kOutput, calls=%fused_computation.102.clone.1 | convolution fusion | flops 849348608 | bytes 40513544 | tf_op jit(solution)/shard_map/while/body/eval_jaxpr/sub | solution.py:75
  349.6 9.8 %fusion.95 = bf16[4,512,6,128]{3,1,2,0:T(8,128)(2,1)} fusion(bf16[4,512,6,128]{3,1,2,0:T(8,128)(2,1)} %get-tuple-element.480, s32[]{:T(128)} %get-tuple-element.479, bf16[2048,6,256]{2,0,1:T(8,128)(2,1)} %get-tuple-element.502, bf16[6,512,2048]{2,1,0:T(8,128)(2,1)} %get-tuple-element.462, f32[512,6]{0,1:T(8,128)S(1)} %bitcast.91), kind=kOutput, calls=%fused_computation.23.clone.1 | convolution fusion | flops 1611399168 | bytes 16527872 | tf_op jit(solution)/shard_map/while/body/eval_jaxpr/hqk,khd->qhd/dot_general | solution.py:77
  361.1 2.5 fusion.92
  363.6 13.9 %fusion.93 = f32[6,512,2048]{2,1,0:T(8,128)} fusion(bf16[2048,6,256]{2,0,1:T(8,128)(2,1)} %get-tuple-element.502, bf16[2048,6,192]{0,2,1:T(8,128)(2,1)} %get-tuple-element.501, s32[]{:T(128)S(6)} %select_n.126), kind=kOutput, calls=%fused_computation.18.clone.1 | convolution fusion | flops 1610612736 | bytes 29097988 | tf_op jit(solution)/shard_map/while/body/eval_jaxpr/qhd,khd->hqk/dot_general | solution.py:64
  377.5 19.2 %fusion.94 = (f32[6,512]{1,0:T(8,128)S(1)}, bf16[6,512,2048]{2,1,0:T(8,128)(2,1)}) fusion(pred[512,2048]{1,0:T(8,128)(4,1)S(1)} %fusion.92, f32[6,512,2048]{2,1,0:T(8,128)} %fusion.93, bf16[2048,6,192]{0,2,1:T(8,128)(2,1)} %get-tuple-element.501, s32[]{:T(128)S(6)} %select_n.126, s32[]{:T(128)S(6)} %add.191, ...), kind=kOutput, calls=%fused_computation.102.clone.1 | convolution fusion | flops 849348608 | bytes 40513544 | tf_op jit(solution)/shard_map/while/body/eval_jaxpr/sub | solution.py:75
  396.7 9.8 %fusion.95 = bf16[4,512,6,128]{3,1,2,0:T(8,128)(2,1)} fusion(bf16[4,512,6,128]{3,1,2,0:T(8,128)(2,1)} %get-tuple-element.480, s32[]{:T(128)} %get-tuple-element.479, bf16[2048,6,256]{2,0,1:T(8,128)(2,1)} %get-tuple-element.502, bf16[6,512,2048]{2,1,0:T(8,128)(2,1)} %get-tuple-element.462, f32[512,6]{0,1:T(8,128)S(1)} %bitcast.91), kind=kOutput, calls=%fused_computation.23.clone.1 | convolution fusion | flops 1611399168 | bytes 16527872 | tf_op jit(solution)/shard_map/while/body/eval_jaxpr/hqk,khd->qhd/dot_general | solution.py:77
  408.2 2.5 fusion.92
  410.7 13.9 %fusion.93 = f32[6,512,2048]{2,1,0:T(8,128)} fusion(bf16[2048,6,256]{2,0,1:T(8,128)(2,1)} %get-tuple-element.502, bf16[2048,6,192]{0,2,1:T(8,128)(2,1)} %get-tuple-element.501, s32[]{:T(128)S(6)} %select_n.126), kind=kOutput, calls=%fused_computation.18.clone.1 | convolution fusion | flops 1610612736 | bytes 29097988 | tf_op jit(solution)/shard_map/while/body/eval_jaxpr/qhd,khd->hqk/dot_general | solution.py:64
  424.6 19.2 %fusion.94 = (f32[6,512]{1,0:T(8,128)S(1)}, bf16[6,512,2048]{2,1,0:T(8,128)(2,1)}) fusion(pred[512,2048]{1,0:T(8,128)(4,1)S(1)} %fusion.92, f32[6,512,2048]{2,1,0:T(8,128)} %fusion.93, bf16[2048,6,192]{0,2,1:T(8,128)(2,1)} %get-tuple-element.501, s32[]{:T(128)S(6)} %select_n.126, s32[]{:T(128)S(6)} %add.191, ...), kind=kOutput, calls=%fused_computation.102.clone.1 | convolution fusion | flops 849348608 | bytes 40513544 | tf_op jit(solution)/shard_map/while/body/eval_jaxpr/sub | solution.py:75
  443.8 9.8 %fusion.95 = bf16[4,512,6,128]{3,1,2,0:T(8,128)(2,1)} fusion(bf16[4,512,6,128]{3,1,2,0:T(8,128)(2,1)} %get-tuple-element.480, s32[]{:T(128)} %get-tuple-element.479, bf16[2048,6,256]{2,0,1:T(8,128)(2,1)} %get-tuple-element.502, bf16[6,512,2048]{2,1,0:T(8,128)(2,1)} %get-tuple-element.462, f32[512,6]{0,1:T(8,128)S(1)} %bitcast.91), kind=kOutput, calls=%fused_computation.23.clone.1 | convolution fusion | flops 1611399168 | bytes 16527872 | tf_op jit(solution)/shard_map/while/body/eval_jaxpr/hqk,khd->qhd/dot_general | solution.py:77
  453.6 6.2 %copy.50 = bf16[4,512,6,128]{1,0,3,2:T(4,128)(2,1)} copy(bf16[4,512,6,128]{3,1,2,0:T(8,128)(2,1)} %get-tuple-element.223) | data formatting | bytes 6291456 | tf_op jit(solution)/shard_map/while | solution.py:174
  459.7 5.7 %all_to_all.14 = bf16[16,128,768]{1,0,2:T(8,128)(2,1)} reshape(bf16[4,512,6,128]{1,0,3,2:T(4,128)(2,1)} %copy.50) | data formatting | bytes 6291456 | tf_op jit(solution)/shard_map/all_to_all | solution.py:176
  465.4 2.7 copy.51
  468.1 44.0 %all_to_all.19 = bf16[16,128,768]{1,2,0:T(8,128)(2,1)} all-to-all(bf16[16,128,768]{1,2,0:T(8,128)(2,1)S(1)} %copy.51), channel_id=1, replica_groups=mesh['batch'=8,'ctx'=16] {'ctx'}, dimensions={0} | all-to-all | bytes 6291456 | tf_op jit(solution)/shard_map/all_to_all | solution.py:176
  512.2 4.6 copy.52
  (88 shorter events, 12.7 us)
Async XLA Ops:
  6.5 76.6 %copy-start = (bf16[128,7168]{1,0:T(8,128)(2,1)S(1)}, bf16[128,7168]{1,0:T(8,128)(2,1)}, u32[]{:S(2)}) copy-start(bf16[128,7168]{1,0:T(8,128)(2,1)} %param.13) | copy-start | bytes 5505028
  6.5 101.6 %all-gather.10.cloned.1.call-start = ((), (), s32[]{:S(2)}) async-start(), calls=%async_computation.3 | async-start | bytes 7397376 | tf_op jit(solution)/shard_map/all_gather | solution.py:113
  7.3 107.2 %all-gather.8.cloned.1.call-start = ((), (), s32[]{:S(2)}) async-start(), calls=%async_computation.2 | async-start | bytes 3981312 | tf_op jit(solution)/shard_map/all_gather | solution.py:136
  8.0 167.3 %all-gather.6.cloned.1.call-start = ((), (), s32[]{:S(2)}) async-start(), calls=%async_computation.1 | async-start | bytes 6684672 | tf_op jit(solution)/shard_map/all_gather | solution.py:140
  8.7 192.4 %all-gather.14.cloned.1.call-start = ((), (), s32[]{:S(2)}) async-start(), calls=%async_computation.5 | async-start | bytes 1769472 | tf_op jit(solution)/shard_map/all_gather | solution.py:137
  9.3 238.7 %all-gather.12.cloned.1.call-start = ((), (), s32[]{:S(2)}) async-start(), calls=%async_computation.4 | async-start | bytes 2228224 | tf_op jit(solution)/shard_map/all_gather | solution.py:132
  108.0 4.4 copy-start.4
  108.1 5.2 copy-start.5
  108.1 5.2 copy-start.6
  256.2 8.7 %copy-start.2 = (s32[1,4]{1,0:T(1,128)S(1)}, s32[1,4]{1,0:T(1,128)}, u32[]{:S(2)}) copy-start(s32[1,4]{1,0:T(1,128)} %param.21) | copy-start | bytes 52
  256.2 8.7 %copy-start.3 = (s32[1,4]{1,0:T(1,128)S(1)}, s32[1,4]{1,0:T(1,128)}, u32[]{:S(2)}) copy-start(s32[1,4]{1,0:T(1,128)} %param.22) | copy-start | bytes 52
  468.1 48.7 %copy-start.1 = (bf16[128,7168]{1,0:T(8,128)(2,1)S(1)}, bf16[128,7168]{1,0:T(8,128)(2,1)}, u32[]{:S(2)}) copy-start(bf16[128,7168]{1,0:T(8,128)(2,1)} %param.13) | copy-start | bytes 5505028
Sparse Core Ops, SparseCore 0:
  10.3 72.6 all-gather.9
  84.7 27.4 all-gather.7
  114.3 60.9 all-gather.5
  176.9 24.2 all-gather.13
  203.1 44.8 all-gather.11
where the time goes:
time: 524 us; the launch traced here: 523 us
  matrix products  196 us (37%)
  blocking collectives  140 us (27%)
  waiting for transfers between devices  122 us (23%)
  local copies, waits for them, and re-layouts  31.1 us (6%)
  other arithmetic  18.3 us (3%)
  between operations  13.3 us (3%)
    sub x4, matrix products, attend(): weights = jnp.where(mask[None], jnp.exp(scores - maxima), 0.0)  76.7 us
    all_gather x1, blocking collectives, per_device(): lax.all_gather(w_down_rope, ('batch', 'ctx'), axis=1, tiled=True)  72.1 us
    all_gather x1, waiting for transfers between devices, per_device(): pieces = lax.all_gather(q_latent, 'ctx', axis=0, tiled=True)  60.9 us
    dot_general x4, matrix products, attend(): jnp.einsum('qhd,khd->hqk', query_tile[..., :NOPE], key_nope, preferred_el...  55.7 us
    all_gather x1, waiting for transfers between devices, per_device(): lax.all_gather(kv_normed, 'ctx', axis=0, tiled=True)  46.9 us
    all_to_all x1, blocking collectives, per_device(): lax.all_to_all(outputs, 'ctx', split_axis=0, concat_axis=1, tiled=True)  44 us
    dot_general x4, matrix products, attend(): jnp.einsum('hqk,khd->qhd', weights.astype(jnp.bfloat16), values, preferre...  39 us
    all_gather x1, blocking collectives, per_device(): lax.all_gather(key_rope, 'ctx', axis=1, tiled=True)  23.8 us
  transfers between devices with their start and end apart: 5, of which 3 were waited for; matrix products, arithmetic and copies ran while one was open for 4% of the time, Pallas kernels for 0%

commit v1 on v0

v1 whole, which is shorter than its diff:
```python
import functools
import math

import jax
import jax.numpy as jnp
from jax import lax
from jax.experimental import pallas as pl
from jax.experimental.pallas import tpu as pltpu
from jax.sharding import PartitionSpec as P

NOPE = 128
ROPE = 64
VDIM = 128
BLK = 128
HL = 6
NB = 16
PAD = 3 * BLK
PACK = NB * BLK
MESH = pl.DeviceIdType.MESH
EXP_SCALE = (NOPE + ROPE) ** (-0.5) * math.log2(math.e)
LOW = -1e30
NT = (((1,), (1,)), ((), ()))


def shifted(c, i):
    return ((c // 4 + i // 4) % 4) * 4 + (c % 4 + i % 4) % 4


def attend_block(t, tab_ref, q_ref, kv_ref, kr_ref, write):
    start, window, anchor = tab_ref[t, 0], tab_ref[t, 1], tab_ref[t, 2]
    bias = []
    for j in range(4):
        kb = t - 3 + j
        ok = (kb >= start) & ((window > 3 - j) | (kb == anchor))
        bias.append(jnp.where(ok, 0.0, LOW))
    bias.append(jnp.where((anchor >= 0) & (anchor < t - 3), 0.0, LOW))
    first = pl.multiple_of(t * BLK, BLK)
    near_blocks, far = pl.ds(t, 4), tab_ref[t, 3]
    causal = lax.broadcasted_iota(jnp.int32, (BLK, BLK), 0) >= lax.broadcasted_iota(
        jnp.int32, (BLK, BLK), 1
    )
    for h in range(HL):
        qh = jnp.concatenate(
            [
                q_ref[pl.ds(first, BLK), h * BLK : (h + 1) * BLK],
                q_ref[pl.ds(first, BLK), (HL + h // 2) * BLK : (HL + h // 2 + 1) * BLK],
            ],
            axis=1,
        )
        part = (h % 2) * BLK
        kcol, vcol = 2 * h * BLK, (2 * h + 1) * BLK
        kn = jnp.concatenate(
            [kv_ref[near_blocks, :, kcol : kcol + BLK], kr_ref[near_blocks, :, part : part + BLK]],
            axis=2,
        ).reshape(4 * BLK, 2 * BLK)
        kf = jnp.concatenate(
            [kv_ref[far, :, kcol : kcol + BLK], kr_ref[far, :, part : part + BLK]], axis=1
        )
        near = lax.dot_general(qh, kn, NT, preferred_element_type=jnp.float32)
        tiles = [near[:, j * BLK : (j + 1) * BLK] for j in range(4)]
        tiles[3] = jnp.where(causal, tiles[3], LOW)
        tiles.append(lax.dot_general(qh, kf, NT, preferred_element_type=jnp.float32))
        top = tiles[0] + bias[0]
        for j in range(1, 5):
            top = jnp.maximum(top, tiles[j] + bias[j])
        top = jnp.max(top, axis=1, keepdims=True) * EXP_SCALE
        weights = [jnp.exp2(tiles[j] * EXP_SCALE - (top - bias[j])) for j in range(5)]
        total = weights[0]
        for j in range(1, 5):
            total = total + weights[j]
        total = jnp.sum(total, axis=1, keepdims=True)
        wn = jnp.concatenate([w.astype(jnp.bfloat16) for w in weights[:4]], axis=1)
        mixed = jnp.dot(
            wn,
            kv_ref[near_blocks, :, vcol : vcol + BLK].reshape(4 * BLK, BLK),
            preferred_element_type=jnp.float32,
        ) + jnp.dot(
            weights[4].astype(jnp.bfloat16),
            kv_ref[far, :, vcol : vcol + BLK],
            preferred_element_type=jnp.float32,
        )
        write(h, (mixed / total).astype(jnp.bfloat16))


def attention_kernel(tab_ref, q_ref, kv_ref, kr_ref, o_ref, obuf, ssem, rsem):
    c = lax.axis_index("ctx")
    barrier = pltpu.get_barrier_semaphore()
    for i in range(1, NB):
        pl.semaphore_signal(barrier, inc=1, device_id={"ctx": shifted(c, i)}, device_id_type=MESH)
    pl.semaphore_wait(barrier, NB - 1)

    own = pl.ds(pl.multiple_of(c * HL * BLK, HL * BLK), HL * BLK)

    def remote(i):
        return pltpu.make_async_remote_copy(
            src_ref=obuf.at[i],
            dst_ref=o_ref.at[:, own],
            send_sem=ssem.at[i],
            recv_sem=rsem.at[i],
            device_id={"ctx": shifted(c, i)},
            device_id_type=MESH,
        )

    def work(i):
        t = shifted(c, i)

        def write(h, value):
            obuf[i, :, h * BLK : (h + 1) * BLK] = value

        attend_block(t, tab_ref, q_ref, kv_ref, kr_ref, write)

    def step(i, carry):
        work(i)
        remote(i).start()
        return carry

    lax.fori_loop(1, NB, step, 0)
    work(0)
    local = pltpu.make_async_copy(obuf.at[0], o_ref.at[:, own], ssem.at[0])
    local.start()
    local.wait()

    def finish(i, carry):
        remote(i).wait()
        return carry

    lax.fori_loop(1, NB, finish, 0)


def attention(tab, q, kv, kr):
    return pl.pallas_call(
        attention_kernel,
        name="attention",
        out_shape=jax.ShapeDtypeStruct((BLK, NB * HL * VDIM), jnp.bfloat16),
        in_specs=[pl.BlockSpec(memory_space=pltpu.SMEM)]
        + [pl.BlockSpec(memory_space=pltpu.VMEM)] * 3,
        out_specs=pl.BlockSpec(memory_space=pl.ANY),
        scratch_shapes=[
            pltpu.VMEM((NB, BLK, HL * VDIM), jnp.bfloat16),
            pltpu.SemaphoreType.DMA((NB,)),
            pltpu.SemaphoreType.DMA((NB,)),
        ],
        compiler_params=pltpu.CompilerParams(
            collective_id=1, has_side_effects=True, vmem_limit_bytes=40 * 2**20
        ),
    )(tab, q, kv, kr)


def angles(positions):
    half_dim = ROPE // 2
    freq = jnp.exp(-math.log(10000.0) * 2.0 * jnp.arange(half_dim, dtype=jnp.float32) / ROPE)
    phase = positions[:, None] * freq[None, :]
    return (jnp.cos(phase), jnp.sin(phase))


def rotate(values, cosine, sine):
    half_dim = ROPE // 2
    first = values[..., :half_dim]
    second = values[..., half_dim:]
    return jnp.concatenate(
        [first * cosine - second * sine, first * sine + second * cosine], axis=-1
    )


def rotate_rows(values, cosine, sine):
    half_dim = ROPE // 2
    first = values[:half_dim]
    second = values[half_dim:]
    return jnp.concatenate([first * cosine - second * sine, first * sine + second * cosine], axis=0)


def block_table(stream_len, window, flags, pick):
    ends = jnp.cumsum(stream_len)
    starts = ends - stream_len
    anchors = jnp.where(flags == 1, starts + pick % stream_len, -1)
    blocks = jnp.arange(NB, dtype=jnp.int32)
    inside = (starts[None, :] <= blocks[:, None]) & (blocks[:, None] < ends[None, :])
    rows = jnp.stack([starts, window, anchors, jnp.maximum(anchors, 0) + 3], axis=1)
    return jnp.sum(jnp.where(inside[:, :, None], rows[None], 0), axis=1).astype(jnp.int32)


def per_device(
    tokens,
    q_latent,
    w_down_kv,
    w_down_rope,
    kv_gain,
    w_up_q,
    w_up_kv,
    lengths,
    window,
    flags,
    anchor_pick,
):
    ctx_index = lax.axis_index("ctx")
    table = block_table(lengths[0], window[0], flags[0], anchor_pick[0])

    latent = jnp.dot(
        tokens,
        lax.all_gather(w_down_kv, ("batch", "ctx"), axis=0, tiled=True),
        preferred_element_type=jnp.float32,
    )
    rope_part = lax.dot_general(
        lax.all_gather(w_down_rope, ("batch", "ctx"), axis=1, tiled=True),
        tokens,
        (((1,), (1,)), ((), ())),
        preferred_element_type=jnp.float32,
    )
    row_ids = jnp.arange(PACK, dtype=jnp.int32)
    row_cos, row_sin = angles(
        (row_ids - jnp.repeat(table[:, 0], BLK, total_repeat_length=PACK) * BLK).astype(jnp.float32)
    )
    cosine = lax.dynamic_slice_in_dim(row_cos, ctx_index * BLK, BLK, 0)
    sine = lax.dynamic_slice_in_dim(row_sin, ctx_index * BLK, BLK, 0)
    kv_normed = (
        latent * lax.rsqrt(jnp.mean(latent * latent, axis=-1, keepdims=True) + 1e-06) * kv_gain
    ).astype(jnp.bfloat16)
    key_rope = rotate_rows(rope_part, jnp.transpose(cosine), jnp.transpose(sine)).astype(
        jnp.bfloat16
    )
    kv_all, rope_all = (
        lax.all_gather(kv_normed, "ctx", axis=0, tiled=True),
        lax.all_gather(key_rope, "ctx", axis=1, tiled=True),
    )
    split = w_up_q.reshape(-1, HL, NOPE + ROPE)
    split = jnp.concatenate(
        [split[:, :, :NOPE].reshape(-1, HL * NOPE), split[:, :, NOPE:].reshape(-1, HL * ROPE)], axis=1
    )
    query_up, keyval_up = (
        lax.all_gather(split, "batch", axis=0, tiled=True),
        lax.all_gather(w_up_kv, "batch", axis=0, tiled=True),
    )
    pieces = lax.all_gather(q_latent, "ctx", axis=0, tiled=True)
    projected = jnp.dot(pieces, query_up, preferred_element_type=jnp.float32)
    turned = rotate(
        projected[:, HL * NOPE :].reshape(PACK, HL, ROPE), row_cos[:, None, :], row_sin[:, None, :]
    ).reshape(PACK, HL * ROPE)
    query = jnp.concatenate([projected[:, : HL * NOPE], turned], axis=1).astype(jnp.bfloat16)
    keyval = jnp.dot(kv_all, keyval_up, preferred_element_type=jnp.float32).astype(jnp.bfloat16)
    rope_rows = rope_all.T
    none = jnp.zeros_like(rope_rows)
    kr = jnp.concatenate([rope_rows, none, none, rope_rows], axis=1)
    keyval = jnp.pad(keyval, ((PAD, 0), (0, 0)))
    kr = jnp.pad(kr, ((PAD, 0), (0, 0)))
    return attention(
        table, query, keyval.reshape(NB + 3, BLK, -1), kr.reshape(NB + 3, BLK, 2 * BLK)
    )


def solution(mesh):
    return jax.shard_map(
        per_device,
        mesh=mesh,
        in_specs=(
            P(("batch", "ctx"), None),
            P(("batch", "ctx"), None),
            P(("batch", "ctx"), None),
            P(None, ("batch", "ctx")),
            P(),
            P("batch", "ctx"),
            P("batch", "ctx"),
            P("batch", None),
            P("batch", None),
            P("batch", None),
            P("batch", None),
        ),
        out_specs=P(("batch", "ctx"), None),
        check_vma=False,
    )
```

time: 524 us -> 332 us (0.63)
  matrix products: 196 us -> 24.6 us
  Pallas kernels: 0 us -> 60 us
  blocking collectives: 140 us -> 94.9 us
  waiting for transfers between devices: 122 us -> 97 us
  local copies, waits for them, and re-layouts: 31.1 us -> 20.1 us
    dot_general x10 -> x2, matrix products: 110 us -> 15.7 us  [the longest x1 11.4 us: per_device(): projected = jnp.dot(pieces, query_up, preferred_element_type=jnp.float32)]
    sub x4 -> x0, matrix products: 76.7 us -> none  [attend(): weights = jnp.where(mask[None], jnp.exp(scores - maxima), 0.0)]
    pallas_call x0 -> x1, Pallas kernels: none -> 60 us  [attention(): pl.pallas_call(attention_kernel, name='attention', out_shape=jax.ShapeDty...]
    all_to_all x1 -> x0, blocking collectives: 44 us -> none  [per_device(): lax.all_to_all(outputs, 'ctx', split_axis=0, concat_axis=1, tiled=True)]
    all_to_all x3 -> x0, local copies, waits for them, and re-layouts: 13 us -> none  [per_device(): lax.all_to_all(outputs, 'ctx', split_axis=0, concat_axis=1, tiled=True)]
    all_gather x1, waiting for transfers between devices: 11.3 us -> 0.01 us  [per_device(): lax.all_gather(w_up_kv, 'batch', axis=0, tiled=True)]
    all_gather x1, waiting for transfers between devices: 60.9 us -> 50.2 us  [per_device(): pieces = lax.all_gather(q_latent, 'ctx', axis=0, tiled=True)]
    and x4 -> x1, other arithmetic: 9.82 us -> 0.07 us  [block_table(): (starts[None, :] <= blocks[:, None]) & (blocks[:, None] < ends[None, :])]
  transfers between devices with their start and end apart: 5 -> 5, of which waited for: 3 -> 2; matrix products, arithmetic and copies ran while one was open for 4% -> 15% of each run, Pallas kernels for 0% -> 0%
where the time goes in v1:
time: 332 us; the launch traced here: 331 us
  waiting for transfers between devices  97 us (29%)
  blocking collectives  94.9 us (29%)
  Pallas kernels  60 us (18%)
  matrix products  24.6 us (7%)
  other arithmetic  21.1 us (6%)
  local copies, waits for them, and re-layouts  20.1 us (6%)
  between operations  13.4 us (4%)
    all_gather x1, blocking collectives, per_device(): lax.all_gather(w_down_rope, ('batch', 'ctx'), axis=1, tiled=True)  70.6 us
    pallas_call x1, Pallas kernels, attention(): pl.pallas_call(attention_kernel, name='attention', out_shape=jax.ShapeDty...  60 us
    all_gather x1, waiting for transfers between devices, per_device(): pieces = lax.all_gather(q_latent, 'ctx', axis=0, tiled=True)  50.2 us
    all_gather x1, waiting for transfers between devices, per_device(): lax.all_gather(kv_normed, 'ctx', axis=0, tiled=True)  44.8 us
    all_gather x1, blocking collectives, per_device(): lax.all_gather(key_rope, 'ctx', axis=1, tiled=True)  24.3 us
    dot_general x1, matrix products, per_device(): projected = jnp.dot(pieces, query_up, preferred_element_type=jnp.float32)  11.4 us
    dot_general x1, matrix products, per_device(): jnp.dot(kv_all, keyval_up, preferred_element_type=jnp.float32)  8.16 us
  transfers between devices with their start and end apart: 5, of which 2 were waited for; matrix products, arithmetic and copies ran while one was open for 15% of the time, Pallas kernels for 0%

profile of v1, /device:TPU:0, one launch (start us, length us, event | category | flops | bytes accessed | tf_op | source)
XLA Modules:
  0.0 331.3 jit_solution(6612212328886736794)
XLA Ops:
  6.5 0.7 all-gather.10.cloned.1.call-update
  7.3 1.2 copy.28
  8.8 0.2 copy.38
  9.0 0.8 pad_maximum_fusion.3
  9.9 0.7 all-gather.8.cloned.1.call-update
  10.6 0.5 all-gather.14.cloned.1.call-update
  11.2 0.2 reduce-window.9
  11.8 0.7 fusion.12
  12.5 4.5 %compare_select_fusion.1 = (s32[2048,1]{0,1:T(1,128)S(1)}, s32[2048,1]{0,1:T(1,128)S(1)}) fusion(s32[]{:T(128)} %bitcast.25, s32[]{:T(128)} %bitcast.26, s32[]{:T(128)} %bitcast.27, s32[]{:T(128)} %bitcast.28, s32[]{:T(128)} %bitcast.29, s32[]{:T(128)} %bitcast.31, s32[]{:T(128)} %bitcast.30, s32[2048,1]{0,1:T(1,128)S(1)} %bitcast.95, s32[2048,1]{0,1:T(1,128)S(1)} %bitcast.96), kind=kLoop, calls=%fused_computation.23 | loop fusion | flops 28672 | bytes 32796 | tf_op jit(solution)/shard_map/jit(_take)/gather | solution.py:211
  17.0 0.2 compare_reduce_fusion.8
  17.2 5.7 %fusion.6 = f32[2048]{0:T(1024)S(1)} fusion(pred[2048]{0:T(1024)(128)(4,1)S(1)} %get-tuple-element.25, pred[2048]{0:T(1024)(128)(4,1)S(1)} %get-tuple-element.24, pred[2048]{0:T(1024)(128)(4,1)S(1)} %get-tuple-element.23, pred[2048]{0:T(1024)(128)(4,1)S(1)} %get-tuple-element.22, pred[2048]{0:T(1024)(128)(4,1)S(1)} %get-tuple-element.21, ...), kind=kLoop, calls=%fused_computation.42 | loop fusion | flops 43008 | bytes 34852 | tf_op jit(solution)/shard_map/convert_element_type | solution.py:211
  22.9 70.6 %all_gather.26 = bf16[64,7168]{0,1:T(8,128)(2,1)S(1)} all-gather(bf16[64,56]{0,1:T(8,128)(2,1)S(1)} %copy-done.5), channel_id=1, replica_groups=mesh['batch'=8,'ctx'=16] {'batch','ctx'}, dimensions={1}, use_global_device_ids=true | all-gather | bytes 924672 | tf_op jit(solution)/shard_map/all_gather | solution.py:204
  93.6 0.7 fusion.13
  94.3 1.0 multiply_cosine_fusion
  95.3 24.3 %all_gather.27 = bf16[64,2048]{1,0:T(8,128)(2,1)S(1)} all-gather(bf16[64,128]{1,0:T(8,128)(2,1)S(1)} %pad_maximum_fusion.4), channel_id=1, replica_groups=mesh['batch'=8,'ctx'=16] {'ctx'}, dimensions={1}, use_global_device_ids=true | all-gather | bytes 278528 | tf_op jit(solution)/shard_map/all_gather | solution.py:223
  119.6 0.3 copy.34
  120.0 4.3 %multiply_reduce_fusion = (f32[128]{0:T(128)S(1)}, f32[128,512]{1,0:T(8,128)S(1)}) fusion(bf16[128,7168]{1,0:T(8,128)(2,1)S(1)} %copy-done, bf16[7168,512]{1,0:T(8,128)(2,1)} %all-gather.10.cloned.1.call-done), kind=kOutput, calls=%fused_computation.12 | convolution fusion | flops 939655040 | bytes 9437696 | tf_op jit(solution)/shard_map/dot_general | solution.py:198
  124.3 0.7 multiply_convert_fusion
  125.0 0.3 pad_maximum_fusion.2
  125.6 50.2 %all-gather.8.cloned.1.call-done = bf16[2048,1536]{1,0:T(8,128)(2,1)} async-done(((bf16[128,1536]{1,0:T(8,128)(2,1)}), bf16[2048,1536]{1,0:T(8,128)(2,1)}) %all-gather.8.cloned.1.call-update) | async-done | bytes 6291472 | tf_op jit(solution)/shard_map/all_gather | solution.py:233
  175.8 11.4 %convolution_bitcast_fusion = f32[2048,1152]{1,0:T(8,128)S(1)} fusion(bf16[2048,1536]{1,0:T(8,128)(2,1)} %all-gather.8.cloned.1.call-done, bf16[1536,1152]{1,0:T(8,128)(2,1)} %all-gather.6.cloned.1.call-done), kind=kOutput, calls=%fused_computation | convolution fusion | flops 7247757312 | bytes 19267584 | tf_op jit(solution)/shard_map/dot_general | solution.py:234
  187.2 1.9 slice.107
  189.1 2.0 slice.121
  191.0 3.6 %copy.32 = f32[2048,384]{0,1:T(8,128)} copy(f32[2048,384]{1,0:T(8,128)} %slice.107) | data formatting | bytes 6291456 | tf_op jit(solution)/shard_map/slice | solution.py:236
  194.7 2.4 subtract_convert_fusion
  197.2 1.6 copy.33
  198.8 4.9 %pad_maximum_fusion.q_ref = bf16[2048,1152]{1,0:T(8,128)(2,1)} fusion(bf16[2048,384]{1,0:T(8,128)(2,1)} %copy.33, bf16[2048,768]{1,0:T(8,128)(2,1)} %slice.121), kind=kLoop, calls=%fused_computation.3 | loop fusion | flops 9437184 | bytes 9437184 | tf_op jit(solution)/shard_map/concatenate | solution.py:238
  203.6 44.8 %all-gather.12.cloned.1.call-done = bf16[2048,512]{1,0:T(8,128)(2,1)} async-done(((bf16[128,512]{1,0:T(8,128)(2,1)}), bf16[2048,512]{1,0:T(8,128)(2,1)}) %all-gather.12.cloned.1.call-update) | async-done | bytes 2097168 | tf_op jit(solution)/shard_map/all_gather | solution.py:222
  248.5 8.2 %convolution_convert_fusion = bf16[2048,1536]{1,0:T(8,128)(2,1)} fusion(bf16[2048,512]{1,0:T(8,128)(2,1)} %all-gather.12.cloned.1.call-done, bf16[512,1536]{1,0:T(8,128)(2,1)} %all-gather.14.cloned.1.call-done), kind=kOutput, calls=%fused_computation.1 | convolution fusion | flops 3224371200 | bytes 9961472 | tf_op jit(solution)/shard_map/dot_general | solution.py:239
  256.6 6.4 %pad.11 = bf16[2432,1536]{1,0:T(8,128)(2,1)} pad(bf16[2048,1536]{1,0:T(8,128)(2,1)} %convolution_convert_fusion, bf16[]{:T(256)} %constant.110.clone.1), padding=384_0x0_0 | pad | bytes 13762562 | tf_op jit(solution)/shard_map/jit(_pad)/pad | solution.py:243
  263.0 60.0 %attention.1 = bf16[128,12288]{1,0:T(8,128)(2,1)S(1)} custom-call(s32[16,4]{1,0:T(8,128)S(1)} %copy.36.tab_ref, bf16[2048,1152]{1,0:T(8,128)(2,1)S(1)} %copy-done.2, bf16[19,128,1536]{2,1,0:T(8,128)(2,1)} %bitcast.86, bf16[19,128,256]{2,1,0:T(8,128)(2,1)S(1)} %bitcast.85), custom_call_target="tpu_custom_call" | custom-call | tf_op jit(solution)/shard_map/attention/pallas_call | solution.py:131
  323.1 1.7 copy.40
  (52 shorter events, 1.2 us)
Async XLA Ops:
  6.5 87.0 %copy-start = (bf16[128,7168]{1,0:T(8,128)(2,1)S(1)}, bf16[128,7168]{1,0:T(8,128)(2,1)}, u32[]{:S(2)}) copy-start(bf16[128,7168]{1,0:T(8,128)(2,1)} %param.13) | copy-start | bytes 5505028
  6.5 113.4 %all-gather.10.cloned.1.call-start = ((), (), s32[]{:S(2)}) async-start(), calls=%async_computation.2 | async-start | bytes 7397376 | tf_op jit(solution)/shard_map/all_gather | solution.py:200
  7.3 118.3 %all-gather.6.cloned.1.call-start = ((), (), s32[]{:S(2)}) async-start(), calls=%async_computation | async-start | bytes 3981312 | tf_op jit(solution)/shard_map/all_gather | solution.py:230
  8.6 2.6 copy-start.8
  8.6 2.8 copy-start.7
  8.6 2.8 copy-start.9
  8.6 2.9 copy-start.10
  8.6 14.3 %copy-start.5 = (bf16[64,56]{0,1:T(8,128)(2,1)S(1)}, bf16[64,56]{0,1:T(8,128)(2,1)}, u32[]{:S(2)}) copy-start(bf16[64,56]{0,1:T(8,128)(2,1)} %param.16) | copy-start | bytes 21508
  9.8 166.0 %all-gather.8.cloned.1.call-start = ((), (), s32[]{:S(2)}) async-start(), calls=%async_computation.1 | async-start | bytes 6684672 | tf_op jit(solution)/shard_map/all_gather | solution.py:233
  10.5 193.1 %all-gather.14.cloned.1.call-start = ((), (), s32[]{:S(2)}) async-start(), calls=%async_computation.4 | async-start | bytes 1769472 | tf_op jit(solution)/shard_map/all_gather | solution.py:231
  11.1 237.3 %all-gather.12.cloned.1.call-start = ((), (), s32[]{:S(2)}) async-start(), calls=%async_computation.3 | async-start | bytes 2228224 | tf_op jit(solution)/shard_map/all_gather | solution.py:222
  95.2 24.3 %copy-start.3 = (f32[2048,32]{0,1:T(8,128)}, f32[2048,32]{0,1:T(8,128)S(1)}, u32[]{:S(2)}) copy-start(f32[2048,32]{0,1:T(8,128)S(1)} %get-tuple-element.35) | copy-start | bytes 786436
  120.0 4.3 %copy-start.6 = (f32[512]{0:T(512)S(1)}, f32[512]{0:T(512)}, u32[]{:S(2)}) copy-start(f32[512]{0:T(512)} %param.17) | copy-start | bytes 6148
  191.0 3.6 %copy-start.4 = (f32[2048,32]{0,1:T(8,128)S(1)}, f32[2048,32]{0,1:T(8,128)}, u32[]{:S(2)}) copy-start(f32[2048,32]{0,1:T(8,128)} %copy-done.3) | copy-start | bytes 786436
  256.6 6.4 %copy-start.2 = (bf16[2048,1152]{1,0:T(8,128)(2,1)S(1)}, bf16[2048,1152]{1,0:T(8,128)(2,1)}, u32[]{:S(2)}) copy-start(bf16[2048,1152]{1,0:T(8,128)(2,1)} %pad_maximum_fusion.q_ref) | copy-start | bytes 14155780
  263.0 61.7 %copy-start.1 = (bf16[128,7168]{1,0:T(8,128)(2,1)S(1)}, bf16[128,7168]{1,0:T(8,128)(2,1)}, u32[]{:S(2)}) copy-start(bf16[128,7168]{1,0:T(8,128)(2,1)} %param.13) | copy-start | bytes 5505028
Sparse Core Ops, SparseCore 0:
  10.3 72.5 all-gather.9
  84.6 27.9 all-gather.5
  114.8 60.9 all-gather.7
  177.3 24.2 all-gather.13
  203.6 44.8 all-gather.11

commit v2 on v1

v2 whole, which is shorter than its diff:
```python
import functools
import math

import jax
import jax.numpy as jnp
import numpy as np
from jax import lax
from jax.experimental import pallas as pl
from jax.experimental.pallas import tpu as pltpu
from jax.sharding import PartitionSpec as P

NOPE = 128
ROPE = 64
VDIM = 128
BLK = 128
HALF = BLK // 2
HL = 6
NB = 16
MOST = 8
KVL = 512
QL = 1536
D = 7168
SHARD = D // 128
SPAN = NB * SHARD
WQ = HL * (NOPE + ROPE)
WKV = HL * (NOPE + VDIM)
KVR = KVL + 2 * ROPE
MESH = pl.DeviceIdType.MESH
EXP_SCALE = (NOPE + ROPE) ** (-0.5) * math.log2(math.e)
LOW = -1e30
NT = (((1,), (1,)), ((), ()))
F32 = jnp.float32
BF16 = jnp.bfloat16
PARTS = ((0, 256, "xyz"), (256, 512, "yzx"), (512, 640, "zxy"))


def shifted(c, i):
    return ((c // 4 + i // 4) % 4) * 4 + (c % 4 + i % 4) % 4


class Ring:
    def __init__(self, block, half, me, plus, minus, ssem, rsem, base):
        def copy(ref, device, k):
            return pltpu.make_async_remote_copy(
                src_ref=ref,
                dst_ref=ref,
                send_sem=ssem.at[base + k],
                recv_sem=rsem.at[base + k],
                device_id=device,
                device_id_type=MESH,
            )

        self.up = copy(block(me), plus, 0)
        self.down = copy(block(me), minus, 1)
        self.on_up = copy(half((me + 3) % 4, 0), plus, 2)
        self.on_down = copy(half((me + 1) % 4, 1), minus, 3)

    def start(self):
        self.up.start()
        self.down.start()

    def middle(self):
        self.up.wait_recv()
        self.on_up.start()
        self.down.wait_recv()
        self.on_down.start()

    def end(self):
        self.on_up.wait_recv()
        self.on_down.wait_recv()

    def sent(self):
        for c in (self.up, self.down, self.on_up, self.on_down):
            c.wait_send()


def turn(v, cosine, sine):
    lane = lax.broadcasted_iota(jnp.int32, v.shape, 1)
    other = jnp.where(lane % 64 < 32, pltpu.roll(v, 96, 1), pltpu.roll(v, 32, 1))
    return v * cosine + other * sine


def attend_block(t, tab_ref, q_ref, kv_ref, kr_ref, write):
    start, window, anchor = tab_ref[t, 0], tab_ref[t, 1], tab_ref[t, 2]
    bias = []
    for j in range(4):
        kb = t - 3 + j
        ok = (kb >= start) & ((window > 3 - j) | (kb == anchor))
        bias.append(jnp.where(ok, 0.0, LOW))
    bias.append(jnp.where((anchor >= 0) & (anchor < t - 3), 0.0, LOW))
    near_blocks, far = pl.ds(t, 4), tab_ref[t, 3]
    causal = lax.broadcasted_iota(jnp.int32, (BLK, BLK), 0) >= lax.broadcasted_iota(
        jnp.int32, (BLK, BLK), 1
    )
    for h in range(HL):
        qh = jnp.concatenate(
            [
                q_ref[t, :, h * BLK : (h + 1) * BLK],
                q_ref[t, :, (HL + h // 2) * BLK : (HL + h // 2 + 1) * BLK],
            ],
            axis=1,
        )
        part = (h % 2) * BLK
        kcol, vcol = 2 * h * BLK, (2 * h + 1) * BLK
        kn = jnp.concatenate(
            [kv_ref[near_blocks, :, kcol : kcol + BLK], kr_ref[near_blocks, :, part : part + BLK]],
            axis=2,
        ).reshape(4 * BLK, 2 * BLK)
        kf = jnp.concatenate(
            [kv_ref[far, :, kcol : kcol + BLK], kr_ref[far, :, part : part + BLK]], axis=1
        )
        near = lax.dot_general(qh, kn, NT, preferred_element_type=F32)
        tiles = [near[:, j * BLK : (j + 1) * BLK] for j in range(4)]
        tiles[3] = jnp.where(causal, tiles[3], LOW)
        tiles.append(lax.dot_general(qh, kf, NT, preferred_element_type=F32))
        top = tiles[0] + bias[0]
        for j in range(1, 5):
            top = jnp.maximum(top, tiles[j] + bias[j])
        top = jnp.max(top, axis=1, keepdims=True) * EXP_SCALE
        weights = [jnp.exp2(tiles[j] * EXP_SCALE - (top - bias[j])) for j in range(5)]
        total = weights[0]
        for j in range(1, 5):
            total = total + weights[j]
        total = jnp.sum(total, axis=1, keepdims=True)
        wn = jnp.concatenate([w.astype(BF16) for w in weights[:4]], axis=1)
        mixed = jnp.dot(
            wn,
            kv_ref[near_blocks, :, vcol : vcol + BLK].reshape(4 * BLK, BLK),
            preferred_element_type=F32,
        ) + jnp.dot(
            weights[4].astype(BF16),
            kv_ref[far, :, vcol : vcol + BLK],
            preferred_element_type=F32,
        )
        write(h, (mixed / total).astype(BF16))


def spread(tok_ref, col, store):
    lane = lax.broadcasted_iota(jnp.int32, (BLK, BLK), 1)
    for p in range(8):
        tile, off = divmod(2 * SHARD * p, BLK)
        v = tok_ref[:, pl.ds(col + tile * BLK, BLK)].astype(F32)
        if off:
            v = pltpu.roll(v, BLK - off, 1)
            if tile < 6:
                after = tok_ref[:, pl.ds(col + (tile + 1) * BLK, BLK)].astype(F32)
                v = jnp.where(lane < BLK - off, v, pltpu.roll(after, BLK - off, 1))
        store(p, jnp.where(lane < 64, v, pltpu.roll(v, 8, 1)).astype(BF16))


def kernel(
    tab_ref,
    tok_ref,
    ql_ref,
    wd_ref,
    wq_ref,
    wkv_ref,
    gain_ref,
    cos_ref,
    sin_ref,
    o_ref,
    wd_a,
    wd_b,
    wd_c,
    ql_a,
    ql_b,
    kvn_a,
    kvn_b,
    wq,
    wkv,
    tok,
    tok_out,
    part,
    part_in,
    q,
    kv,
    kr,
    obuf,
    ssem,
    rsem,
    csem,
    cother,
    asem,
    arem,
):
    b, c = lax.axis_index("batch"), lax.axis_index("ctx")
    z, core, y, x = b // 2, b % 2, c // 4, c % 4
    at = {"x": x, "y": y, "z": z}

    def neighbour(axis, by):
        if axis == "x":
            return {"ctx": y * 4 + (x + by) % 4}
        if axis == "y":
            return {"ctx": ((y + by) % 4) * 4 + x}
        return {"batch": ((z + by) % 4) * 2 + core}

    partner = {"batch": z * 2 + 1 - core}

    barrier = pltpu.get_barrier_semaphore()
    peers = [{"ctx": shifted(c, i)} for i in range(1, NB)]
    peers += [neighbour("z", 1), neighbour("z", 3), partner]
    for peer in peers:
        pl.semaphore_signal(barrier, inc=1, device_id=peer, device_id_type=MESH)

    used = [0]

    def ring(axis, block, half):
        base = used[0]
        used[0] += 4
        return Ring(
            block, half, at[axis], neighbour(axis, 1), neighbour(axis, 3), ssem, rsem, base
        )

    def gather(buf, order, mid, dims="yx"):
        stages = []
        for i, axis in enumerate(order):
            done = order[:i]

            def block(k, axis=axis, done=done):
                index = [k if a == axis else slice(None) if a in done else at[a] for a in dims]
                return buf.at[tuple(index)]

            def half(k, h, axis=axis, done=done):
                index = [k if a == axis else slice(None) if a in done else at[a] for a in dims]
                return buf.at[tuple(index) + (pl.ds(h * mid, mid),)]

            stages.append(ring(axis, block, half))
        return stages

    def swap(src, dst, k):
        return pltpu.make_async_remote_copy(
            src_ref=src,
            dst_ref=dst,
            send_sem=csem.at[k],
            recv_sem=cother.at[k],
            device_id=partner,
            device_id_type=MESH,
        )

    wd_buf = (wd_a, wd_b, wd_c)
    wd = [gather(buf, order, 32, "zyx") for buf, (_, _, order) in zip(wd_buf, PARTS)]
    ql = [gather(ql_a, "xy", 32), gather(ql_b, "yx", 32)]
    kvn = [gather(kvn_a, "xy", 32), gather(kvn_b, "yx", 32)]

    def up_ring(buf, rows):
        return ring(
            "z",
            lambda k: buf.at[k, core],
            lambda k, h: buf.at[k, core, pl.ds(h * rows // 2, rows // 2)],
        )

    wq_ring, wkv_ring = up_ring(wq, QL // 8), up_ring(wkv, KVL // 8)

    for buf, (lo, hi, _) in zip(wd_buf, PARTS):
        buf[z, y, x] = wd_ref[:, lo:hi]
    ql_a[y, x] = ql_ref[:HALF]
    ql_b[y, x] = ql_ref[HALF:]
    wkv[z, core] = wkv_ref[...]
    wq[z, core] = wq_ref[...]

    pl.semaphore_wait(barrier, len(peers))
    for g in wd:
        g[0].start()
    for g in ql:
        g[0].start()
    wkv_ring.start()

    def spread_out(i, carry):
        def keep(p, v):
            tok[i, 0, :, p * BLK : (p + 1) * BLK] = v

        def give(p, v):
            tok_out[i, :, p * BLK : (p + 1) * BLK] = v

        spread(tok_ref, pl.multiple_of((i * 2 + core) * SPAN, BLK), keep)
        spread(tok_ref, pl.multiple_of((i * 2 + 1 - core) * SPAN, BLK), give)
        return carry

    for g in wd:
        g[0].middle()
    lax.fori_loop(0, 4, spread_out, 0)
    tok_swap = swap(tok_out, tok.at[:, 1], 0)
    tok_swap.start()
    for g in wd:
        g[0].end()
        g[1].start()
    for g in ql:
        g[0].middle()
    for g in wd:
        g[1].middle()
    for g in wd:
        g[1].end()
        g[2].start()
    for g in ql:
        g[0].end()
        g[1].start()
    wkv_ring.middle()
    wq_ring.start()

    kv[0:3] = jnp.zeros((3, BLK, WKV), BF16)
    kr[0:3] = jnp.zeros((3, BLK, 2 * BLK), BF16)

    for g in wd:
        g[2].middle()
    wkv_ring.end()
    wkv_swap = [swap(wkv.at[i, core], wkv.at[i, core], 1 + i) for i in range(4)]
    for s in wkv_swap:
        s.start()
    tok_swap.wait_recv()
    for g in wd:
        g[2].end()

    def down(i, carry):
        t = tok[i].reshape(2 * BLK, 8 * BLK)
        for buf, (lo, hi, _) in zip(wd_buf, PARTS):
            w = buf[i].reshape(NB * 64, hi - lo)
            part[:, :, lo:hi] += jnp.dot(t, w, preferred_element_type=F32).reshape(2, BLK, hi - lo)
        return carry

    part[...] = jnp.zeros_like(part)
    lax.fori_loop(0, 4, down, 0)
    part_swap = swap(part.at[1], part_in, 5)
    part_swap.start()
    for g in ql:
        g[1].middle()
    wq_ring.middle()
    part_swap.wait_recv()
    both = part[0] + part_in[...]
    latent = both[:, :KVL]
    norm = lax.rsqrt(jnp.mean(latent * latent, axis=1, keepdims=True) + 1e-06)
    place = tab_ref[c, 4]
    own = jnp.concatenate(
        [latent * norm * gain_ref[...], turn(both[:, KVL:], cos_ref[place], sin_ref[place])], axis=1
    ).astype(BF16)
    kvn_a[y, x] = own[:HALF]
    kvn_b[y, x] = own[HALF:]
    for g in kvn:
        g[0].start()
    wq_ring.end()
    wq_swap = [swap(wq.at[i, core], wq.at[i, core], 6 + i) for i in range(4)]
    for s in wq_swap:
        s.start()
    for g in kvn:
        g[0].middle()
    for g in kvn:
        g[0].end()
        g[1].start()
    for g in ql:
        g[1].end()
    for g in kvn:
        g[1].middle()
    for s in wq_swap:
        s.wait_recv()

    def queries(buf, row):
        rows = slice(row, row + HALF)

        def body(i, carry):
            left = buf[i].reshape(4 * HALF, QL)
            weight = wq[...].reshape(QL, WQ)
            plain = jnp.dot(left, weight[:, : HL * NOPE], preferred_element_type=F32)
            q[pl.ds(4 * i, 4), rows, : HL * NOPE] = plain.astype(BF16).reshape(4, HALF, HL * NOPE)
            rope = jnp.dot(left, weight[:, HL * NOPE :], preferred_element_type=F32)
            for k in range(4):
                t = 4 * i + k
                place = tab_ref[t, 4]
                cosine, sine = cos_ref[place, rows], sin_ref[place, rows]
                for j in range(HL // 2):
                    v = rope[k * HALF : (k + 1) * HALF, j * BLK : (j + 1) * BLK]
                    lo = (HL + j) * BLK
                    q[t, rows, lo : lo + BLK] = turn(v, cosine, sine).astype(BF16)
            return carry

        lax.fori_loop(0, 4, body, 0)

    queries(ql_a, 0)
    queries(ql_b, HALF)
    for g in kvn:
        g[1].end()
    for s in wkv_swap:
        s.wait_recv()

    lane = lax.broadcasted_iota(jnp.int32, (4, HALF, BLK), 2)

    def keyvals(buf, row):
        rows = slice(row, row + HALF)

        def body(i, carry):
            left = buf[i]
            weight = wkv[...].reshape(KVL, WKV)
            blocks = pl.ds(3 + 4 * i, 4)
            value = jnp.dot(
                left[:, :, :KVL].reshape(4 * HALF, KVL), weight, preferred_element_type=F32
            )
            kv[blocks, rows, :] = value.astype(BF16).reshape(4, HALF, WKV)
            turned = left[:, :, KVL:].astype(F32)
            kr[blocks, rows, :BLK] = jnp.where(lane < ROPE, turned, 0.0).astype(BF16)
            kr[blocks, rows, BLK:] = jnp.where(lane < ROPE, 0.0, turned).astype(BF16)
            return carry

        lax.fori_loop(0, 4, body, 0)

    keyvals(kvn_a, 0)
    keyvals(kvn_b, HALF)

    columns = pl.ds(pl.multiple_of(c * HL * BLK, HL * BLK), HL * BLK)

    def remote(i):
        return pltpu.make_async_remote_copy(
            src_ref=obuf.at[i],
            dst_ref=o_ref.at[:, columns],
            send_sem=asem.at[i],
            recv_sem=arem.at[i],
            device_id={"ctx": shifted(c, i)},
            device_id_type=MESH,
        )

    def work(i):
        def write(h, value):
            obuf[i, :, h * BLK : (h + 1) * BLK] = value

        attend_block(shifted(c, i), tab_ref, q, kv, kr, write)

    def step(i, carry):
        work(i)
        remote(i).start()
        return carry

    lax.fori_loop(1, NB, step, 0)
    work(0)
    local = pltpu.make_async_copy(obuf.at[0], o_ref.at[:, columns], asem.at[0])
    local.start()
    for g in wd + ql + kvn + [[wq_ring, wkv_ring]]:
        for s in g:
            s.sent()
    for s in [tok_swap, part_swap] + wkv_swap + wq_swap:
        s.wait_send()
    local.wait()

    def finish(i, carry):
        remote(i).wait()
        return carry

    lax.fori_loop(1, NB, finish, 0)


def tables():
    freq = np.exp(-math.log(10000.0) * 2.0 * np.arange(32, dtype=np.float32) / ROPE).astype(np.float32)
    phase = np.arange(MOST * BLK, dtype=np.float32)[:, None] * freq[None, :]
    cosine, sine = np.cos(phase.astype(np.float64)), np.sin(phase.astype(np.float64))
    shape = (MOST, BLK, BLK)
    return (
        np.concatenate([cosine] * 4, axis=1).astype(np.float32).reshape(shape),
        np.concatenate([-sine, sine, -sine, sine], axis=1).astype(np.float32).reshape(shape),
    )


def block_table(stream_len, window, flags, pick):
    slots = jnp.arange(4, dtype=jnp.int32)
    starts = jnp.sum(jnp.where(slots[None, :] < slots[:, None], stream_len[None, :], 0), axis=1)
    anchors = jnp.where(flags == 1, starts + pick % stream_len, -1)
    blocks = jnp.arange(NB, dtype=jnp.int32)
    inside = (starts[None, :] <= blocks[:, None]) & (
        blocks[:, None] < (starts + stream_len)[None, :]
    )
    rows = jnp.stack([starts, window, anchors, jnp.maximum(anchors, 0) + 3], axis=1)
    rows = jnp.concatenate(
        [jnp.broadcast_to(rows[None], (NB, 4, 4)), (blocks[:, None] - starts[None, :])[:, :, None]],
        axis=2,
    )
    return jnp.sum(jnp.where(inside[:, :, None], rows, 0), axis=1).astype(jnp.int32)


def per_device(
    tokens,
    q_latent,
    w_down_kv,
    w_down_rope,
    kv_gain,
    w_up_q,
    w_up_kv,
    lengths,
    window,
    flags,
    anchor_pick,
):
    table = block_table(lengths[0], window[0], flags[0], anchor_pick[0])
    rope = w_down_rope.T
    wd = jnp.pad(jnp.concatenate([w_down_kv, rope, rope], axis=1), ((0, 64 - SHARD), (0, 0)))
    split = w_up_q.reshape(-1, HL, NOPE + ROPE)
    wq = jnp.concatenate(
        [split[:, :, :NOPE].reshape(-1, HL * NOPE), split[:, :, NOPE:].reshape(-1, HL * ROPE)], axis=1
    )
    cosine, sine = tables()
    vmem = pl.BlockSpec(memory_space=pltpu.VMEM)
    n_sem = 4 * 19
    return pl.pallas_call(
        kernel,
        name="mla",
        out_shape=jax.ShapeDtypeStruct((BLK, NB * HL * VDIM), BF16),
        in_specs=[pl.BlockSpec(memory_space=pltpu.SMEM)] + [vmem] * 8,
        out_specs=pl.BlockSpec(memory_space=pl.ANY),
        scratch_shapes=[
            pltpu.VMEM((4, 4, 4, 64, 256), BF16),
            pltpu.VMEM((4, 4, 4, 64, 256), BF16),
            pltpu.VMEM((4, 4, 4, 64, 128), BF16),
            pltpu.VMEM((4, 4, HALF, QL), BF16),
            pltpu.VMEM((4, 4, HALF, QL), BF16),
            pltpu.VMEM((4, 4, HALF, KVR), BF16),
            pltpu.VMEM((4, 4, HALF, KVR), BF16),
            pltpu.VMEM((4, 2, QL // 8, WQ), BF16),
            pltpu.VMEM((4, 2, KVL // 8, WKV), BF16),
            pltpu.VMEM((4, 2, BLK, 8 * BLK), BF16),
            pltpu.VMEM((4, BLK, 8 * BLK), BF16),
            pltpu.VMEM((2, BLK, KVR), F32),
            pltpu.VMEM((BLK, KVR), F32),
            pltpu.VMEM((NB, BLK, WQ), BF16),
            pltpu.VMEM((NB + 3, BLK, WKV), BF16),
            pltpu.VMEM((NB + 3, BLK, 2 * BLK), BF16),
            pltpu.VMEM((NB, BLK, HL * VDIM), BF16),
            pltpu.SemaphoreType.DMA((n_sem,)),
            pltpu.SemaphoreType.DMA((n_sem,)),
            pltpu.SemaphoreType.DMA((10,)),
            pltpu.SemaphoreType.DMA((10,)),
            pltpu.SemaphoreType.DMA((NB,)),
            pltpu.SemaphoreType.DMA((NB,)),
        ],
        compiler_params=pltpu.CompilerParams(
            collective_id=1, has_side_effects=True, vmem_limit_bytes=56 * 2**20
        ),
    )(table, tokens, q_latent, wd, wq, w_up_kv, kv_gain.reshape(1, KVL), cosine, sine)


def solution(mesh):
    return jax.shard_map(
        per_device,
        mesh=mesh,
        in_specs=(
            P(("batch", "ctx"), None),
            P(("batch", "ctx"), None),
            P(("batch", "ctx"), None),
            P(None, ("batch", "ctx")),
            P(),
            P("batch", "ctx"),
            P("batch", "ctx"),
            P("batch", None),
            P("batch", None),
            P("batch", None),
            P("batch", None),
        ),
        out_specs=P(("batch", "ctx"), None),
        check_vma=False,
    )
```

time: 332 us -> 165 us (0.50)
  waiting for transfers between devices: 97 us -> 0 us
  blocking collectives: 94.9 us -> 0 us
  Pallas kernels: 60 us -> 153 us
  matrix products: 24.6 us -> 0 us
  other arithmetic: 21.1 us -> 5.44 us
  local copies, waits for them, and re-layouts: 20.1 us -> 6.15 us
  between operations: 13.4 us -> 0.05 us
    all_gather x5 -> x0, waiting for transfers between devices: 95 us -> none  [the longest x1 50.2 us: per_device(): pieces = lax.all_gather(q_latent, 'ctx', axis=0, tiled=True)]
    all_gather x2 -> x0, blocking collectives: 94.9 us -> none  [the longest x1 70.6 us: per_device(): lax.all_gather(w_down_rope, ('batch', 'ctx'), axis=1, tiled=True)]
    pallas_call x1, Pallas kernels: 60 us -> 153 us  [per_device(): pl.pallas_call(kernel, name='mla', out_shape=jax.ShapeDtypeStruct((BLK, N...]
    dot_general x4 -> x0, matrix products: 24.6 us -> none  [the longest x1 11.4 us: per_device(): projected = jnp.dot(pieces, query_up, preferred_element_type=jnp.float32)]
    slice x3 -> x0, local copies, waits for them, and re-layouts: 7.46 us -> none  [the longest x2 5.49 us: per_device(): projected[:, HL * NOPE:].reshape(PACK, HL, ROPE)]
    pad x2 -> x0, local copies, waits for them, and re-layouts: 6.5 us -> none  [the longest x1 6.42 us: per_device(): keyval = jnp.pad(keyval, ((PAD, 0), (0, 0)))]
    convert_element_type x2 -> x0, other arithmetic: 6.4 us -> none  [the longest x1 5.66 us: per_device(): (row_ids - jnp.repeat(table[:, 0], BLK, total_repeat_length=PACK) * BLK)....]
    gather x2 -> x0, other arithmetic: 4.68 us -> none  [per_device(): jnp.repeat(table[:, 0], BLK, total_repeat_length=PACK) * BLK]
  transfers between devices with their start and end apart: 5 -> 0, of which waited for: 2 -> 0; matrix products, arithmetic and copies ran while one was open for 15% -> 0% of each run, Pallas kernels for 0% -> 0%
where the time goes in v2:
time: 165 us; the launch traced here: 164 us
  Pallas kernels  153 us (93%)
  local copies, waits for them, and re-layouts  6.15 us (4%)
  other arithmetic  5.44 us (3%)
    pallas_call x1, Pallas kernels, per_device(): pl.pallas_call(kernel, name='mla', out_shape=jax.ShapeDtypeStruct((BLK, N...  153 us
    unnamed x2, local copies, waits for them, and re-layouts  5.08 us

profile of v2, /device:TPU:0, one launch (start us, length us, event | category | flops | bytes accessed | tf_op | source)
XLA Modules:
  0.0 164.3 jit_solution(6657754311452362111)
XLA Ops:
  0.0 0.8 select_reduce_fusion
  0.8 0.7 fusion.8
  1.4 0.1 fusion.6
  1.5 0.8 maximum_add_fusion
  2.3 0.7 pad_add_fusion
  3.0 0.1 iota_subtract_fusion
  3.1 0.1 broadcast_in_dim.51
  3.2 0.7 copy.29.tab_ref
  3.8 1.6 fusion.4.wd_ref
  5.4 1.2 copy.26
  6.7 0.2 copy.30
  6.9 0.1 copy.28
  7.0 0.8 pad_maximum_fusion.wq_ref
  7.8 152.7 %mla.1 = bf16[128,12288]{1,0:T(8,128)(2,1)} custom-call(s32[16,5]{1,0:T(8,128)} %copy.29.tab_ref, bf16[128,7168]{1,0:T(8,128)(2,1)} %tok_ref.1, bf16[128,1536]{1,0:T(8,128)(2,1)} %ql_ref.1, bf16[64,640]{1,0:T(8,128)(2,1)} %fusion.4.wd_ref, bf16[192,1152]{1,0:T(8,128)(2,1)} %pad_maximum_fusion.wq_ref, bf16[64,1536]{1,0:T(8,128)(2,1)} %wkv_ref.1, ...), custom_call_target="tpu_custom_call" | custom-call | tf_op jit(solution)/shard_map/mla/pallas_call | solution.py:497
  160.5 3.8 %copy.32 = bf16[128,12288]{1,0:T(8,128)(2,1)} copy(bf16[128,12288]{1,0:T(8,128)(2,1)} %mla.1) | data formatting | bytes 6291456
  (3 shorter events, 0.1 us)

commit v3 on v2

--- a/solution.py
+++ b/solution.py
@@ -31,7 +31,8 @@
 NT = (((1,), (1,)), ((), ()))
 F32 = jnp.float32
 BF16 = jnp.bfloat16
-PARTS = ((0, 256, "xyz"), (256, 512, "yzx"), (512, 640, "zxy"))
+ORDERS = ("xyz", "yzx", "zxy")
+PIECE = 96
 
 
 def shifted(c, i):
@@ -72,6 +73,60 @@
     def sent(self):
         for c in (self.up, self.down, self.on_up, self.on_down):
             c.wait_send()
+
+
+class Direct:
+    def __init__(self, block, me, others, ssem, rsem, base):
+        ref = block(me)
+        self.copies = [
+            pltpu.make_async_remote_copy(
+                src_ref=ref,
+                dst_ref=ref,
+                send_sem=ssem.at[base + k],
+                recv_sem=rsem.at[base + k],
+                device_id=other,
+                device_id_type=MESH,
+            )
+            for k, other in enumerate(others)
+        ]
+
+    def start(self):
+        for c in self.copies:
+            c.start()
+
+    def middle(self):
+        pass
+
+    def end(self):
+        for c in self.copies:
+            c.wait_recv()
+
+    def sent(self):
+        for c in self.copies:
+            c.wait_send()
+
+
+def block_table(len_ref, window_ref, flag_ref, pick_ref, tab_ref):
+    starts, anchors, start = [], [], 0
+    for s in range(4):
+        length, rest = len_ref[0, s], pick_ref[0, s]
+        for k in range(16, -1, -1):
+            rest = jnp.where(rest >= length * 2**k, rest - length * 2**k, rest)
+        anchors.append(jnp.where(flag_ref[0, s] == 1, start + rest, -1))
+        starts.append(start)
+        start = start + length
+    for t in range(NB):
+        row = [0, window_ref[0, 0], anchors[0]]
+        for s in range(1, 4):
+            later = starts[s] <= t
+            row = [
+                jnp.where(later, new, old)
+                for new, old in zip((starts[s], window_ref[0, s], anchors[s]), row)
+            ]
+        for k in range(3):
+            tab_ref[t, k] = row[k]
+        tab_ref[t, 3] = jnp.clip(row[2], 0, NB - 1) + 3
+        tab_ref[t, 4] = jnp.clip(t - row[0], 0, MOST - 1)
 
 
 def turn(v, cosine, sine):
@@ -149,10 +204,14 @@
 
 
 def kernel(
-    tab_ref,
+    len_ref,
+    window_ref,
+    flag_ref,
+    pick_ref,
     tok_ref,
     ql_ref,
     wd_ref,
+    wr_ref,
     wq_ref,
     wkv_ref,
     gain_ref,
@@ -176,6 +235,7 @@
     kv,
     kr,
     obuf,
+    tab_ref,
     ssem,
     rsem,
     csem,
@@ -198,7 +258,7 @@
 
     barrier = pltpu.get_barrier_semaphore()
     peers = [{"ctx": shifted(c, i)} for i in range(1, NB)]
-    peers += [neighbour("z", 1), neighbour("z", 3), partner]
+    peers += [neighbour("z", 1), neighbour("z", 2), neighbour("z", 3), partner]
     for peer in peers:
         pl.semaphore_signal(barrier, inc=1, device_id=peer, device_id_type=MESH)
 
@@ -211,7 +271,12 @@
             block, half, at[axis], neighbour(axis, 1), neighbour(axis, 3), ssem, rsem, base
         )
 
-    def gather(buf, order, mid, dims="yx"):
+    def direct(axis, block):
+        base = used[0]
+        used[0] += 4
+        return Direct(block, at[axis], [neighbour(axis, k) for k in (1, 2, 3)], ssem, rsem, base)
+
+    def gather(buf, order, mid, dims="yx", quick=0):
         stages = []
         for i, axis in enumerate(order):
             done = order[:i]
@@ -224,7 +289,7 @@
                 index = [k if a == axis else slice(None) if a in done else at[a] for a in dims]
                 return buf.at[tuple(index) + (pl.ds(h * mid, mid),)]
 
-            stages.append(ring(axis, block, half))
+            stages.append(direct(axis, block) if i < quick else ring(axis, block, half))
         return stages
 
     def swap(src, dst, k):
@@ -238,9 +303,9 @@
         )
 
     wd_buf = (wd_a, wd_b, wd_c)
-    wd = [gather(buf, order, 32, "zyx") for buf, (_, _, order) in zip(wd_buf, PARTS)]
+    wd = [gather(buf, order, PIECE // 2, "zyx", 2) for buf, order in zip(wd_buf, ORDERS)]
     ql = [gather(ql_a, "xy", 32), gather(ql_b, "yx", 32)]
-    kvn = [gather(kvn_a, "xy", 32), gather(kvn_b, "yx", 32)]
+    kvn = [gather(kvn_a, "xy", 32, quick=1), gather(kvn_b, "yx", 32, quick=1)]
 
     def up_ring(buf, rows):
         return ring(
@@ -251,13 +316,30 @@
 
     wq_ring, wkv_ring = up_ring(wq, QL // 8), up_ring(wkv, KVL // 8)
 
-    for buf, (lo, hi, _) in zip(wd_buf, PARTS):
-        buf[z, y, x] = wd_ref[:, lo:hi]
+    down_rows = jnp.concatenate([wd_ref[...].astype(F32), jnp.zeros((64 - SHARD, KVL), F32)], axis=0)
+    rope_rows = lax.dot_general(
+        (
+            lax.broadcasted_iota(jnp.int32, (64, SHARD), 0)
+            == lax.broadcasted_iota(jnp.int32, (64, SHARD), 1)
+        ).astype(F32).astype(BF16),
+        jnp.concatenate([wr_ref[...], wr_ref[...]], axis=0),
+        NT,
+        preferred_element_type=F32,
+    )
+    lane = lax.broadcasted_iota(jnp.int32, (32, BLK), 1)
+    pieces = (
+        (down_rows[:, :128], down_rows[:32, 128:256]),
+        (down_rows[:, 256:384], down_rows[32:, 128:256]),
+        (down_rows[:, 384:], jnp.where(lane < 64, rope_rows[:32], rope_rows[32:])),
+    )
+    for buf, piece in zip(wd_buf, pieces):
+        buf[z, y, x] = jnp.concatenate(piece, axis=0).astype(BF16)
     ql_a[y, x] = ql_ref[:HALF]
     ql_b[y, x] = ql_ref[HALF:]
     wkv[z, core] = wkv_ref[...]
     wq[z, core] = wq_ref[...]
 
+    block_table(len_ref, window_ref, flag_ref, pick_ref, tab_ref)
     pl.semaphore_wait(barrier, len(peers))
     for g in wd:
         g[0].start()
@@ -312,9 +394,20 @@
 
     def down(i, carry):
         t = tok[i].reshape(2 * BLK, 8 * BLK)
-        for buf, (lo, hi, _) in zip(wd_buf, PARTS):
-            w = buf[i].reshape(NB * 64, hi - lo)
-            part[:, :, lo:hi] += jnp.dot(t, w, preferred_element_type=F32).reshape(2, BLK, hi - lo)
+        first, second, third = (buf[i].reshape(NB, PIECE, BLK) for buf in wd_buf)
+        shared = jnp.concatenate([first[:, 64:], second[:, 64:]], axis=1)
+        packed = third[:, 64:].astype(F32)
+        moved = pltpu.roll(packed.reshape(NB * 32, BLK), 64, 1).reshape(NB, 32, BLK)
+        rope = jnp.concatenate([packed, moved], axis=1).astype(BF16)
+        for lo, w in (
+            (0, jnp.concatenate([first[:, :64], shared], axis=2)),
+            (256, jnp.concatenate([second[:, :64], third[:, :64]], axis=2)),
+            (512, rope),
+        ):
+            w = w.reshape(NB * 64, -1)
+            part[:, :, lo : lo + w.shape[1]] += jnp.dot(
+                t, w, preferred_element_type=F32
+            ).reshape(2, BLK, -1)
         return carry
 
     part[...] = jnp.zeros_like(part)
@@ -329,8 +422,11 @@
     latent = both[:, :KVL]
     norm = lax.rsqrt(jnp.mean(latent * latent, axis=1, keepdims=True) + 1e-06)
     place = tab_ref[c, 4]
+    lane = lax.broadcasted_iota(jnp.int32, (BLK, BLK), 1)
+    rope = both[:, KVL:]
+    rope = jnp.where(lane < ROPE, rope, pltpu.roll(rope, 64, 1))
     own = jnp.concatenate(
-        [latent * norm * gain_ref[...], turn(both[:, KVL:], cos_ref[place], sin_ref[place])], axis=1
+        [latent * norm * gain_ref[...], turn(rope, cos_ref[place], sin_ref[place])], axis=1
     ).astype(BF16)
     kvn_a[y, x] = own[:HALF]
     kvn_b[y, x] = own[HALF:]
@@ -352,23 +448,27 @@
     for s in wq_swap:
         s.wait_recv()
 
+    wide = lax.broadcasted_iota(jnp.int32, (4 * HALF, BLK), 1)
+
     def queries(buf, row):
         rows = slice(row, row + HALF)
 
         def body(i, carry):
             left = buf[i].reshape(4 * HALF, QL)
-            weight = wq[...].reshape(QL, WQ)
-            plain = jnp.dot(left, weight[:, : HL * NOPE], preferred_element_type=F32)
-            q[pl.ds(4 * i, 4), rows, : HL * NOPE] = plain.astype(BF16).reshape(4, HALF, HL * NOPE)
-            rope = jnp.dot(left, weight[:, HL * NOPE :], preferred_element_type=F32)
-            for k in range(4):
-                t = 4 * i + k
-                place = tab_ref[t, 4]
-                cosine, sine = cos_ref[place, rows], sin_ref[place, rows]
-                for j in range(HL // 2):
-                    v = rope[k * HALF : (k + 1) * HALF, j * BLK : (j + 1) * BLK]
-                    lo = (HL + j) * BLK
-                    q[t, rows, lo : lo + BLK] = turn(v, cosine, sine).astype(BF16)
+            flat = jnp.dot(left, wq[...].reshape(QL, WQ), preferred_element_type=F32)
+            blocks = pl.ds(4 * i, 4)
+
+            def put(slot, v):
+                q[blocks, rows, slot * BLK : (slot + 1) * BLK] = v.astype(BF16).reshape(4, HALF, BLK)
+
+            places = [tab_ref[4 * i + k, 4] for k in range(4)]
+            cosine = jnp.concatenate([cos_ref[p, rows] for p in places], axis=0)
+            sine = jnp.concatenate([sin_ref[p, rows] for p in places], axis=0)
+            for j in range(HL // 2):
+                one, two, three = (flat[:, k * BLK : (k + 1) * BLK] for k in range(3 * j, 3 * j + 3))
+                put(2 * j, one)
+                put(2 * j + 1, jnp.where(wide < 64, pltpu.roll(two, 64, 1), pltpu.roll(three, 64, 1)))
+                put(HL + j, turn(jnp.where(wide < 64, two, three), cosine, sine))
             return carry
 
         lax.fori_loop(0, 4, body, 0)
@@ -453,22 +553,6 @@
         np.concatenate([cosine] * 4, axis=1).astype(np.float32).reshape(shape),
         np.concatenate([-sine, sine, -sine, sine], axis=1).astype(np.float32).reshape(shape),
     )
-
-
-def block_table(stream_len, window, flags, pick):
-    slots = jnp.arange(4, dtype=jnp.int32)
-    starts = jnp.sum(jnp.where(slots[None, :] < slots[:, None], stream_len[None, :], 0), axis=1)
-    anchors = jnp.where(flags == 1, starts + pick % stream_len, -1)
-    blocks = jnp.arange(NB, dtype=jnp.int32)
-    inside = (starts[None, :] <= blocks[:, None]) & (
-        blocks[:, None] < (starts + stream_len)[None, :]
-    )
-    rows = jnp.stack([starts, window, anchors, jnp.maximum(anchors, 0) + 3], axis=1)
-    rows = jnp.concatenate(
-        [jnp.broadcast_to(rows[None], (NB, 4, 4)), (blocks[:, None] - starts[None, :])[:, :, None]],
-        axis=2,
-    )
-    return jnp.sum(jnp.where(inside[:, :, None], rows, 0), axis=1).astype(jnp.int32)
 
 
 def per_device(
@@ -484,13 +568,6 @@
     flags,
     anchor_pick,
 ):
-    table = block_table(lengths[0], window[0], flags[0], anchor_pick[0])
-    rope = w_down_rope.T
-    wd = jnp.pad(jnp.concatenate([w_down_kv, rope, rope], axis=1), ((0, 64 - SHARD), (0, 0)))
-    split = w_up_q.reshape(-1, HL, NOPE + ROPE)
-    wq = jnp.concatenate(
-        [split[:, :, :NOPE].reshape(-1, HL * NOPE), split[:, :, NOPE:].reshape(-1, HL * ROPE)], axis=1
-    )
     cosine, sine = tables()
     vmem = pl.BlockSpec(memory_space=pltpu.VMEM)
     n_sem = 4 * 19
@@ -498,12 +575,12 @@
         kernel,
         name="mla",
         out_shape=jax.ShapeDtypeStruct((BLK, NB * HL * VDIM), BF16),
-        in_specs=[pl.BlockSpec(memory_space=pltpu.SMEM)] + [vmem] * 8,
+        in_specs=[pl.BlockSpec(memory_space=pltpu.SMEM)] * 4 + [vmem] * 9,
         out_specs=pl.BlockSpec(memory_space=pl.ANY),
         scratch_shapes=[
-            pltpu.VMEM((4, 4, 4, 64, 256), BF16),
-            pltpu.VMEM((4, 4, 4, 64, 256), BF16),
-            pltpu.VMEM((4, 4, 4, 64, 128), BF16),
+            pltpu.VMEM((4, 4, 4, PIECE, BLK), BF16),
+            pltpu.VMEM((4, 4, 4, PIECE, BLK), BF16),
+            pltpu.VMEM((4, 4, 4, PIECE, BLK), BF16),
             pltpu.VMEM((4, 4, HALF, QL), BF16),
             pltpu.VMEM((4, 4, HALF, QL), BF16),
             pltpu.VMEM((4, 4, HALF, KVR), BF16),
@@ -518,6 +595,7 @@
             pltpu.VMEM((NB + 3, BLK, WKV), BF16),
             pltpu.VMEM((NB + 3, BLK, 2 * BLK), BF16),
             pltpu.VMEM((NB, BLK, HL * VDIM), BF16),
+            pltpu.SMEM((NB, 8), jnp.int32),
             pltpu.SemaphoreType.DMA((n_sem,)),
             pltpu.SemaphoreType.DMA((n_sem,)),
             pltpu.SemaphoreType.DMA((10,)),
@@ -528,7 +606,21 @@
         compiler_params=pltpu.CompilerParams(
             collective_id=1, has_side_effects=True, vmem_limit_bytes=56 * 2**20
         ),
-    )(table, tokens, q_latent, wd, wq, w_up_kv, kv_gain.reshape(1, KVL), cosine, sine)
+    )(
+        lengths,
+        window,
+        flags,
+        anchor_pick,
+        tokens,
+        q_latent,
+        w_down_kv,
+        w_down_rope,
+        w_up_q,
+        w_up_kv,
+        kv_gain.reshape(1, KVL),
+        cosine,
+        sine,
+    )
 
 
 def solution(mesh):

time: 165 us -> 151 us (0.915)
  Pallas kernels: 153 us -> 145 us
  other arithmetic: 5.44 us -> 0 us
    pallas_call x1, Pallas kernels: 153 us -> 145 us  [per_device(): pl.pallas_call(kernel, name='mla', out_shape=jax.ShapeDtypeStruct((BLK, N...]
    concatenate x2 -> x0, other arithmetic: 2.36 us -> none  [the longest x1 1.56 us: per_device(): jnp.concatenate([w_down_kv, rope, rope], axis=1)]
where the time goes in v3:
time: 151 us; the launch traced here: 150 us
  Pallas kernels  145 us (96%)
  local copies, waits for them, and re-layouts  5.23 us (3%)
    pallas_call x1, Pallas kernels, per_device(): pl.pallas_call(kernel, name='mla', out_shape=jax.ShapeDtypeStruct((BLK, N...  145 us
    unnamed x2, local copies, waits for them, and re-layouts  5.23 us

profile of v3, /device:TPU:0, one launch (start us, length us, event | category | flops | bytes accessed | tf_op | source)
XLA Modules:
  0.0 150.3 jit_solution(14876837004163264695)
XLA Ops:
  0.0 1.4 copy.14.wr_ref
  1.4 145.1 %mla.1 = bf16[128,12288]{1,0:T(8,128)(2,1)} custom-call(s32[1,4]{1,0:T(1,128)} %len_ref.1, s32[1,4]{1,0:T(1,128)} %window_ref.1, s32[1,4]{1,0:T(1,128)} %flag_ref.1, s32[1,4]{1,0:T(1,128)} %pick_ref.1, bf16[128,7168]{1,0:T(8,128)(2,1)} %tok_ref.1, bf16[128,1536]{1,0:T(8,128)(2,1)} %ql_ref.1, bf16[56,512]{1,0:T(8,128)(2,1)} %wd_ref.1, ...), custom_call_target="tpu_custom_call" | custom-call | tf_op jit(solution)/shard_map/mla/pallas_call | solution.py:574
  146.5 3.8 %copy.16 = bf16[128,12288]{1,0:T(8,128)(2,1)} copy(bf16[128,12288]{1,0:T(8,128)(2,1)} %mla.1) | data formatting | bytes 6291456

commit v4 on v3

--- a/solution.py
+++ b/solution.py
@@ -39,6 +39,10 @@
     return ((c // 4 + i // 4) % 4) * 4 + (c % 4 + i % 4) % 4
 
 
+def turns(i):
+    return i * 7 % NB
+
+
 class Ring:
     def __init__(self, block, half, me, plus, minus, ssem, rsem, base):
         def copy(ref, device, k):
@@ -147,47 +151,53 @@
     causal = lax.broadcasted_iota(jnp.int32, (BLK, BLK), 0) >= lax.broadcasted_iota(
         jnp.int32, (BLK, BLK), 1
     )
-    for h in range(HL):
-        qh = jnp.concatenate(
+
+    def score(h):
+        part, column = (h % 2) * BLK, 2 * h * BLK
+        query = jnp.concatenate(
             [
                 q_ref[t, :, h * BLK : (h + 1) * BLK],
                 q_ref[t, :, (HL + h // 2) * BLK : (HL + h // 2 + 1) * BLK],
             ],
             axis=1,
         )
-        part = (h % 2) * BLK
-        kcol, vcol = 2 * h * BLK, (2 * h + 1) * BLK
-        kn = jnp.concatenate(
-            [kv_ref[near_blocks, :, kcol : kcol + BLK], kr_ref[near_blocks, :, part : part + BLK]],
+        near = jnp.concatenate(
+            [
+                kv_ref[near_blocks, :, column : column + BLK],
+                kr_ref[near_blocks, :, part : part + BLK],
+            ],
             axis=2,
         ).reshape(4 * BLK, 2 * BLK)
-        kf = jnp.concatenate(
-            [kv_ref[far, :, kcol : kcol + BLK], kr_ref[far, :, part : part + BLK]], axis=1
+        last = jnp.concatenate(
+            [kv_ref[far, :, column : column + BLK], kr_ref[far, :, part : part + BLK]], axis=1
         )
-        near = lax.dot_general(qh, kn, NT, preferred_element_type=F32)
-        tiles = [near[:, j * BLK : (j + 1) * BLK] for j in range(4)]
+        keys = jnp.concatenate([near, last], axis=0)
+        return lax.dot_general(query, keys, NT, preferred_element_type=F32)
+
+    def weigh(scores):
+        tiles = [scores[:, j * BLK : (j + 1) * BLK] + bias[j] for j in range(5)]
         tiles[3] = jnp.where(causal, tiles[3], LOW)
-        tiles.append(lax.dot_general(qh, kf, NT, preferred_element_type=F32))
-        top = tiles[0] + bias[0]
-        for j in range(1, 5):
-            top = jnp.maximum(top, tiles[j] + bias[j])
-        top = jnp.max(top, axis=1, keepdims=True) * EXP_SCALE
-        weights = [jnp.exp2(tiles[j] * EXP_SCALE - (top - bias[j])) for j in range(5)]
-        total = weights[0]
-        for j in range(1, 5):
-            total = total + weights[j]
-        total = jnp.sum(total, axis=1, keepdims=True)
-        wn = jnp.concatenate([w.astype(BF16) for w in weights[:4]], axis=1)
-        mixed = jnp.dot(
-            wn,
-            kv_ref[near_blocks, :, vcol : vcol + BLK].reshape(4 * BLK, BLK),
-            preferred_element_type=F32,
-        ) + jnp.dot(
-            weights[4].astype(BF16),
-            kv_ref[far, :, vcol : vcol + BLK],
-            preferred_element_type=F32,
+        top = functools.reduce(jnp.maximum, tiles)
+        top = jnp.max(top, axis=1, keepdims=True)
+        weights = [jnp.exp2((tile - top) * EXP_SCALE) for tile in tiles]
+        total = jnp.sum(sum(weights[1:], weights[0]), axis=1, keepdims=True)
+        return jnp.concatenate([w.astype(BF16) for w in weights], axis=1), total
+
+    def mix(h, weights, total):
+        column = (2 * h + 1) * BLK
+        values = jnp.concatenate(
+            [
+                kv_ref[near_blocks, :, column : column + BLK].reshape(4 * BLK, BLK),
+                kv_ref[far, :, column : column + BLK],
+            ],
+            axis=0,
         )
-        write(h, (mixed / total).astype(BF16))
+        return jnp.dot(weights, values, preferred_element_type=F32) / total
+
+    scores = [score(h) for h in range(HL)]
+    weighed = [weigh(s) for s in scores]
+    for h in range(HL):
+        write(h, mix(h, *weighed[h]).astype(BF16))
 
 
 def spread(tok_ref, col, store):
@@ -511,7 +521,7 @@
             dst_ref=o_ref.at[:, columns],
             send_sem=asem.at[i],
             recv_sem=arem.at[i],
-            device_id={"ctx": shifted(c, i)},
+            device_id={"ctx": shifted(c, turns(i))},
             device_id_type=MESH,
         )
 
@@ -519,7 +529,7 @@
         def write(h, value):
             obuf[i, :, h * BLK : (h + 1) * BLK] = value
 
-        attend_block(shifted(c, i), tab_ref, q, kv, kr, write)
+        attend_block(shifted(c, turns(i)), tab_ref, q, kv, kr, write)
 
     def step(i, carry):
         work(i)
@@ -574,9 +584,9 @@
     return pl.pallas_call(
         kernel,
         name="mla",
-        out_shape=jax.ShapeDtypeStruct((BLK, NB * HL * VDIM), BF16),
+        out_shape=pltpu.VMEM((BLK, NB * HL * VDIM), BF16),
         in_specs=[pl.BlockSpec(memory_space=pltpu.SMEM)] * 4 + [vmem] * 9,
-        out_specs=pl.BlockSpec(memory_space=pl.ANY),
+        out_specs=pl.BlockSpec(memory_space=pltpu.VMEM),
         scratch_shapes=[
             pltpu.VMEM((4, 4, 4, PIECE, BLK), BF16),
             pltpu.VMEM((4, 4, 4, PIECE, BLK), BF16),

time: 151 us -> 132 us (0.87)
  Pallas kernels: 145 us -> 129 us
  local copies, waits for them, and re-layouts: 5.23 us -> 3.07 us
    pallas_call x1, Pallas kernels: 145 us -> 129 us  [per_device(): pl.pallas_call(kernel, name='mla', out_shape=pltpu.VMEM((BLK, NB * HL * V...]
    unnamed x2, local copies, waits for them, and re-layouts: 5.23 us -> 3.07 us
where the time goes in v4:
time: 132 us
  Pallas kernels  129 us (98%)
  local copies, waits for them, and re-layouts  3.07 us (2%)
    pallas_call x1, Pallas kernels, per_device(): pl.pallas_call(kernel, name='mla', out_shape=pltpu.VMEM((BLK, NB * HL * V...  129 us
    unnamed x2, local copies, waits for them, and re-layouts  3.07 us

profile of v4, /device:TPU:0, one launch (start us, length us, event | category | flops | bytes accessed | tf_op | source)
XLA Modules:
  0.0 132.1 jit_solution(1444592853525025914)
XLA Ops:
  0.0 1.4 %copy.14.wr_ref = bf16[64,56]{1,0:T(8,128)(2,1)} copy(bf16[64,56]{0,1:T(8,128)(2,1)} %param.16) | data formatting | bytes 14336 | tf_op args[3]
  1.4 129.0 %mla.1 = bf16[128,12288]{1,0:T(8,128)(2,1)S(1)} custom-call(s32[1,4]{1,0:T(1,128)} %len_ref.1, s32[1,4]{1,0:T(1,128)} %window_ref.1, s32[1,4]{1,0:T(1,128)} %flag_ref.1, s32[1,4]{1,0:T(1,128)} %pick_ref.1, bf16[128,7168]{1,0:T(8,128)(2,1)} %tok_ref.1, bf16[128,1536]{1,0:T(8,128)(2,1)} %ql_ref.1, bf16[56,512]{1,0:T(8,128)(2,1)} %wd_ref.1, ...), custom_call_target="tpu_custom_call" | custom-call | tf_op jit(solution)/shard_map/mla/pallas_call | solution.py:584
  130.4 1.7 %copy.16 = bf16[128,12288]{1,0:T(8,128)(2,1)} copy(bf16[128,12288]{1,0:T(8,128)(2,1)S(1)} %mla.1) | data formatting | bytes 6291456

commit v5 on v4

--- a/solution.py
+++ b/solution.py
@@ -39,8 +39,15 @@
     return ((c // 4 + i // 4) % 4) * 4 + (c % 4 + i % 4) % 4
 
 
-def turns(i):
-    return i * 7 % NB
+def turns(n):
+    j = n * 2 % 9
+    near = 4 * (j // 3 + j // 6) + j % 3 + (j % 3) // 2
+    j = (15 - n) % 7
+    a = j // 2
+    a, odd = a + a // 2 - 2 * (a // 3), j % 2
+    far = 4 * (2 * (1 - odd) + a * odd) + a * (1 - odd) + 2 * odd
+    late = n // 9
+    return near * (1 - late) + far * late
 
 
 class Ring:
@@ -383,17 +390,17 @@
     for g in wd:
         g[1].end()
         g[2].start()
+    wkv_ring.middle()
+
+    kv[0:3] = jnp.zeros((3, BLK, WKV), BF16)
+    kr[0:3] = jnp.zeros((3, BLK, 2 * BLK), BF16)
+
+    for g in wd:
+        g[2].middle()
     for g in ql:
         g[0].end()
         g[1].start()
-    wkv_ring.middle()
     wq_ring.start()
-
-    kv[0:3] = jnp.zeros((3, BLK, WKV), BF16)
-    kr[0:3] = jnp.zeros((3, BLK, 2 * BLK), BF16)
-
-    for g in wd:
-        g[2].middle()
     wkv_ring.end()
     wkv_swap = [swap(wkv.at[i, core], wkv.at[i, core], 1 + i) for i in range(4)]
     for s in wkv_swap:
@@ -424,9 +431,6 @@
     lax.fori_loop(0, 4, down, 0)
     part_swap = swap(part.at[1], part_in, 5)
     part_swap.start()
-    for g in ql:
-        g[1].middle()
-    wq_ring.middle()
     part_swap.wait_recv()
     both = part[0] + part_in[...]
     latent = both[:, :KVL]
@@ -442,38 +446,44 @@
     kvn_b[y, x] = own[HALF:]
     for g in kvn:
         g[0].start()
+    for g in kvn:
+        g[0].end()
+        g[1].start()
+    for g in ql:
+        g[1].middle()
+    wq_ring.middle()
     wq_ring.end()
     wq_swap = [swap(wq.at[i, core], wq.at[i, core], 6 + i) for i in range(4)]
     for s in wq_swap:
         s.start()
-    for g in kvn:
-        g[0].middle()
-    for g in kvn:
-        g[0].end()
-        g[1].start()
-    for g in ql:
-        g[1].end()
-    for g in kvn:
-        g[1].middle()
-    for s in wq_swap:
-        s.wait_recv()
+
+    def arrival(me, j):
+        return (me + j + j // 2 - 2 * (j // 3)) % 4
 
     wide = lax.broadcasted_iota(jnp.int32, (4 * HALF, BLK), 1)
 
-    def queries(buf, row):
+    def line(along, j):
+        if along == "y":
+            return [(arrival(y, j), k) for k in range(4)]
+        return [(k, arrival(x, j)) for k in range(4)]
+
+    def queries(buf, row, along, first, last):
         rows = slice(row, row + HALF)
 
-        def body(i, carry):
-            left = buf[i].reshape(4 * HALF, QL)
+        def body(j, carry):
+            places = line(along, j)
+            left = jnp.concatenate([buf[p] for p in places], axis=0)
+            places = [4 * yy + xx for yy, xx in places]
             flat = jnp.dot(left, wq[...].reshape(QL, WQ), preferred_element_type=F32)
-            blocks = pl.ds(4 * i, 4)
 
             def put(slot, v):
-                q[blocks, rows, slot * BLK : (slot + 1) * BLK] = v.astype(BF16).reshape(4, HALF, BLK)
-
-            places = [tab_ref[4 * i + k, 4] for k in range(4)]
-            cosine = jnp.concatenate([cos_ref[p, rows] for p in places], axis=0)
-            sine = jnp.concatenate([sin_ref[p, rows] for p in places], axis=0)
+                v = v.astype(BF16)
+                for k, t in enumerate(places):
+                    q[t, rows, slot * BLK : (slot + 1) * BLK] = v[k * HALF : (k + 1) * HALF]
+
+            turns_of = [tab_ref[t, 4] for t in places]
+            cosine = jnp.concatenate([cos_ref[p, rows] for p in turns_of], axis=0)
+            sine = jnp.concatenate([sin_ref[p, rows] for p in turns_of], axis=0)
             for j in range(HL // 2):
                 one, two, three = (flat[:, k * BLK : (k + 1) * BLK] for k in range(3 * j, 3 * j + 3))
                 put(2 * j, one)
@@ -481,37 +491,45 @@
                 put(HL + j, turn(jnp.where(wide < 64, two, three), cosine, sine))
             return carry
 
-        lax.fori_loop(0, 4, body, 0)
-
-    queries(ql_a, 0)
-    queries(ql_b, HALF)
+        lax.fori_loop(first, last, body, 0)
+
+    lane = lax.broadcasted_iota(jnp.int32, (HALF, BLK), 1)
+
+    def keyvals(buf, row, along, first, last):
+        rows = slice(row, row + HALF)
+
+        def body(j, carry):
+            places = line(along, j)
+            left = [buf[p] for p in places]
+            value = jnp.dot(
+                jnp.concatenate([v[:, :KVL] for v in left], axis=0),
+                wkv[...].reshape(KVL, WKV),
+                preferred_element_type=F32,
+            ).astype(BF16)
+            for k, (yy, xx) in enumerate(places):
+                t = 3 + 4 * yy + xx
+                kv[t, rows, :] = value[k * HALF : (k + 1) * HALF]
+                turned = left[k][:, KVL:].astype(F32)
+                kr[t, rows, :BLK] = jnp.where(lane < ROPE, turned, 0.0).astype(BF16)
+                kr[t, rows, BLK:] = jnp.where(lane < ROPE, 0.0, turned).astype(BF16)
+            return carry
+
+        lax.fori_loop(first, last, body, 0)
+
+    for g in kvn:
+        g[1].middle()
+    for s in wkv_swap:
+        s.wait_recv()
+    keyvals(kvn_a, 0, "y", 0, 3)
+    keyvals(kvn_b, HALF, "x", 0, 3)
+    for s in wq_swap:
+        s.wait_recv()
+    queries(ql_a, 0, "y", 0, 3)
+    queries(ql_b, HALF, "x", 0, 3)
     for g in kvn:
         g[1].end()
-    for s in wkv_swap:
-        s.wait_recv()
-
-    lane = lax.broadcasted_iota(jnp.int32, (4, HALF, BLK), 2)
-
-    def keyvals(buf, row):
-        rows = slice(row, row + HALF)
-
-        def body(i, carry):
-            left = buf[i]
-            weight = wkv[...].reshape(KVL, WKV)
-            blocks = pl.ds(3 + 4 * i, 4)
-            value = jnp.dot(
-                left[:, :, :KVL].reshape(4 * HALF, KVL), weight, preferred_element_type=F32
-            )
-            kv[blocks, rows, :] = value.astype(BF16).reshape(4, HALF, WKV)
-            turned = left[:, :, KVL:].astype(F32)
-            kr[blocks, rows, :BLK] = jnp.where(lane < ROPE, turned, 0.0).astype(BF16)
-            kr[blocks, rows, BLK:] = jnp.where(lane < ROPE, 0.0, turned).astype(BF16)
-            return carry
-
-        lax.fori_loop(0, 4, body, 0)
-
-    keyvals(kvn_a, 0)
-    keyvals(kvn_b, HALF)
+    keyvals(kvn_a, 0, "y", 3, 4)
+    keyvals(kvn_b, HALF, "x", 3, 4)
 
     columns = pl.ds(pl.multiple_of(c * HL * BLK, HL * BLK), HL * BLK)
 
@@ -532,6 +550,13 @@
         attend_block(shifted(c, turns(i)), tab_ref, q, kv, kr, write)
 
     def step(i, carry):
+        @pl.when(i == 9)
+        def _():
+            for g in ql:
+                g[1].end()
+            queries(ql_a, 0, "y", 3, 4)
+            queries(ql_b, HALF, "x", 3, 4)
+
         work(i)
         remote(i).start()
         return carry

time: 132 us -> 126 us (0.955)
  Pallas kernels: 129 us -> 122 us
    pallas_call x1, Pallas kernels: 129 us -> 122 us  [per_device(): pl.pallas_call(kernel, name='mla', out_shape=pltpu.VMEM((BLK, NB * HL * V...]
where the time goes in v5:
time: 126 us; the launch traced here: 125 us
  Pallas kernels  122 us (97%)
  local copies, waits for them, and re-layouts  3.07 us (2%)
    pallas_call x1, Pallas kernels, per_device(): pl.pallas_call(kernel, name='mla', out_shape=pltpu.VMEM((BLK, NB * HL * V...  122 us
    unnamed x2, local copies, waits for them, and re-layouts  3.07 us

profile of v5, /device:TPU:0, one launch (start us, length us, event | category | flops | bytes accessed | tf_op | source)
XLA Modules:
  0.0 125.0 jit_solution(5545650689105953805)
XLA Ops:
  0.0 1.4 %copy.14.wr_ref = bf16[64,56]{1,0:T(8,128)(2,1)} copy(bf16[64,56]{0,1:T(8,128)(2,1)} %param.16) | data formatting | bytes 14336 | tf_op args[3]
  1.4 121.9 %mla.1 = bf16[128,12288]{1,0:T(8,128)(2,1)S(1)} custom-call(s32[1,4]{1,0:T(1,128)} %len_ref.1, s32[1,4]{1,0:T(1,128)} %window_ref.1, s32[1,4]{1,0:T(1,128)} %flag_ref.1, s32[1,4]{1,0:T(1,128)} %pick_ref.1, bf16[128,7168]{1,0:T(8,128)(2,1)} %tok_ref.1, bf16[128,1536]{1,0:T(8,128)(2,1)} %ql_ref.1, bf16[56,512]{1,0:T(8,128)(2,1)} %wd_ref.1, ...), custom_call_target="tpu_custom_call" | custom-call | tf_op jit(solution)/shard_map/mla/pallas_call | solution.py:609
  123.3 1.7 %copy.16 = bf16[128,12288]{1,0:T(8,128)(2,1)} copy(bf16[128,12288]{1,0:T(8,128)(2,1)S(1)} %mla.1) | data formatting | bytes 6291456

commit v6 on v5

--- a/solution.py
+++ b/solution.py
@@ -40,7 +40,7 @@
 
 
 def turns(n):
-    j = n * 2 % 9
+    j = n * 4 % 9
     near = 4 * (j // 3 + j // 6) + j % 3 + (j % 3) // 2
     j = (15 - n) % 7
     a = j // 2
@@ -351,60 +351,56 @@
     )
     for buf, piece in zip(wd_buf, pieces):
         buf[z, y, x] = jnp.concatenate(piece, axis=0).astype(BF16)
-    ql_a[y, x] = ql_ref[:HALF]
-    ql_b[y, x] = ql_ref[HALF:]
-    wkv[z, core] = wkv_ref[...]
-    wq[z, core] = wq_ref[...]
-
-    block_table(len_ref, window_ref, flag_ref, pick_ref, tab_ref)
+
     pl.semaphore_wait(barrier, len(peers))
     for g in wd:
         g[0].start()
+    ql_a[y, x] = ql_ref[:HALF]
+    ql_b[y, x] = ql_ref[HALF:]
     for g in ql:
         g[0].start()
-    wkv_ring.start()
-
-    def spread_out(i, carry):
-        def keep(p, v):
-            tok[i, 0, :, p * BLK : (p + 1) * BLK] = v
-
-        def give(p, v):
-            tok_out[i, :, p * BLK : (p + 1) * BLK] = v
-
-        spread(tok_ref, pl.multiple_of((i * 2 + core) * SPAN, BLK), keep)
-        spread(tok_ref, pl.multiple_of((i * 2 + 1 - core) * SPAN, BLK), give)
-        return carry
-
-    for g in wd:
-        g[0].middle()
-    lax.fori_loop(0, 4, spread_out, 0)
-    tok_swap = swap(tok_out, tok.at[:, 1], 0)
-    tok_swap.start()
     for g in wd:
         g[0].end()
         g[1].start()
+    wkv[z, core] = wkv_ref[...]
+    wq[z, core] = wq_ref[...]
     for g in ql:
         g[0].middle()
-    for g in wd:
-        g[1].middle()
+    block_table(len_ref, window_ref, flag_ref, pick_ref, tab_ref)
     for g in wd:
         g[1].end()
         g[2].start()
-    wkv_ring.middle()
+
+    def give(i, carry):
+        def put(p, v):
+            tok_out[i, :, p * BLK : (p + 1) * BLK] = v
+
+        spread(tok_ref, pl.multiple_of((i * 2 + 1 - core) * SPAN, BLK), put)
+        return carry
+
+    def keep(i, carry):
+        def put(p, v):
+            tok[i, 0, :, p * BLK : (p + 1) * BLK] = v
+
+        spread(tok_ref, pl.multiple_of((i * 2 + core) * SPAN, BLK), put)
+        return carry
+
+    lax.fori_loop(0, 4, give, 0)
+    tok_swap = swap(tok_out, tok.at[:, 1], 0)
+    tok_swap.start()
+    lax.fori_loop(0, 4, keep, 0)
 
     kv[0:3] = jnp.zeros((3, BLK, WKV), BF16)
     kr[0:3] = jnp.zeros((3, BLK, 2 * BLK), BF16)
+
 
     for g in wd:
         g[2].middle()
     for g in ql:
         g[0].end()
         g[1].start()
+    wkv_ring.start()
     wq_ring.start()
-    wkv_ring.end()
-    wkv_swap = [swap(wkv.at[i, core], wkv.at[i, core], 1 + i) for i in range(4)]
-    for s in wkv_swap:
-        s.start()
     tok_swap.wait_recv()
     for g in wd:
         g[2].end()
@@ -431,6 +427,7 @@
     lax.fori_loop(0, 4, down, 0)
     part_swap = swap(part.at[1], part_in, 5)
     part_swap.start()
+    wkv_ring.middle()
     part_swap.wait_recv()
     both = part[0] + part_in[...]
     latent = both[:, :KVL]
@@ -451,6 +448,10 @@
         g[1].start()
     for g in ql:
         g[1].middle()
+    wkv_ring.end()
+    wkv_swap = [swap(wkv.at[i, core], wkv.at[i, core], 1 + i) for i in range(4)]
+    for s in wkv_swap:
+        s.start()
     wq_ring.middle()
     wq_ring.end()
     wq_swap = [swap(wq.at[i, core], wq.at[i, core], 6 + i) for i in range(4)]

time: 126 us -> 124 us (0.984)
  no operation moved by 1% of the time
where the time goes in v6:
time: 124 us
  Pallas kernels  121 us (98%)
  local copies, waits for them, and re-layouts  3.07 us (2%)
    pallas_call x1, Pallas kernels, per_device(): pl.pallas_call(kernel, name='mla', out_shape=pltpu.VMEM((BLK, NB * HL * V...  121 us
    unnamed x2, local copies, waits for them, and re-layouts  3.07 us

profile of v6, /device:TPU:0, one launch (start us, length us, event | category | flops | bytes accessed | tf_op | source)
XLA Modules:
  0.0 124.3 jit_solution(3738633009697983521)
XLA Ops:
  0.0 1.4 %copy.14.wr_ref = bf16[64,56]{1,0:T(8,128)(2,1)} copy(bf16[64,56]{0,1:T(8,128)(2,1)} %param.16) | data formatting | bytes 14336 | tf_op args[3]
  1.4 121.2 %mla.1 = bf16[128,12288]{1,0:T(8,128)(2,1)S(1)} custom-call(s32[1,4]{1,0:T(1,128)} %len_ref.1, s32[1,4]{1,0:T(1,128)} %window_ref.1, s32[1,4]{1,0:T(1,128)} %flag_ref.1, s32[1,4]{1,0:T(1,128)} %pick_ref.1, bf16[128,7168]{1,0:T(8,128)(2,1)} %tok_ref.1, bf16[128,1536]{1,0:T(8,128)(2,1)} %ql_ref.1, bf16[56,512]{1,0:T(8,128)(2,1)} %wd_ref.1, ...), custom_call_target="tpu_custom_call" | custom-call | tf_op jit(solution)/shard_map/mla/pallas_call | solution.py:610
  122.6 1.7 %copy.16 = bf16[128,12288]{1,0:T(8,128)(2,1)} copy(bf16[128,12288]{1,0:T(8,128)(2,1)S(1)} %mla.1) | data formatting | bytes 6291456

commit v7 on v6

--- a/solution.py
+++ b/solution.py
@@ -40,7 +40,7 @@
 
 
 def turns(n):
-    j = n * 4 % 9
+    j = n * 7 % 9
     near = 4 * (j // 3 + j // 6) + j % 3 + (j % 3) // 2
     j = (15 - n) % 7
     a = j // 2

time: 124 us -> 125 us (level)
  no operation moved by 1% of the time
where the time goes in v7:
time: 125 us
  Pallas kernels  122 us (98%)
  local copies, waits for them, and re-layouts  3.07 us (2%)
    pallas_call x1, Pallas kernels, per_device(): pl.pallas_call(kernel, name='mla', out_shape=pltpu.VMEM((BLK, NB * HL * V...  122 us
    unnamed x2, local copies, waits for them, and re-layouts  3.07 us

profile of v7, /device:TPU:0, one launch (start us, length us, event | category | flops | bytes accessed | tf_op | source)
XLA Modules:
  0.0 125.0 jit_solution(16646137332161348091)
XLA Ops:
  0.0 1.4 %copy.14.wr_ref = bf16[64,56]{1,0:T(8,128)(2,1)} copy(bf16[64,56]{0,1:T(8,128)(2,1)} %param.16) | data formatting | bytes 14336 | tf_op args[3]
  1.4 121.9 %mla.1 = bf16[128,12288]{1,0:T(8,128)(2,1)S(1)} custom-call(s32[1,4]{1,0:T(1,128)} %len_ref.1, s32[1,4]{1,0:T(1,128)} %window_ref.1, s32[1,4]{1,0:T(1,128)} %flag_ref.1, s32[1,4]{1,0:T(1,128)} %pick_ref.1, bf16[128,7168]{1,0:T(8,128)(2,1)} %tok_ref.1, bf16[128,1536]{1,0:T(8,128)(2,1)} %ql_ref.1, bf16[56,512]{1,0:T(8,128)(2,1)} %wd_ref.1, ...), custom_call_target="tpu_custom_call" | custom-call | tf_op jit(solution)/shard_map/mla/pallas_call | solution.py:610
  123.3 1.7 %copy.16 = bf16[128,12288]{1,0:T(8,128)(2,1)} copy(bf16[128,12288]{1,0:T(8,128)(2,1)S(1)} %mla.1) | data formatting | bytes 6291456
